TPU v7x, 32 devices: a whole 2x2x4 slice. The times are simulated.
32 devices in a mesh: nodes: 16 (over z, y, core), grp: 2 (over x).
Axes of the slice: x: 2, y: 2, z: 4, core: 2. Of those that a mesh axis runs over, the one named last changes fastest.
Arguments:
- features: float32 [2, 8192, 1024], P('grp', 'nodes'), may hold values from -6 to 6
- type_mask: int32 [2, 8192], P('grp', 'nodes'), may hold values 0 or 1
- edge_child: int32 [2, 409600], P('grp', 'nodes'), may hold values from 0 to 511
- edge_slot: int32 [2, 409600], P('grp', 'nodes'), may hold values from 0 to 2047, as said below
- edge_weight: int32 [2, 409600], P('grp', 'nodes'), may hold values from 1 to 9
- recv_rows: int32 [2, 16, 16, 128], P('grp', 'nodes'), may hold values from 0 to 511
- board_proj: float32 [1024, 1024], replicated, may hold values from -0.1875 to 0.1875
- neigh_proj: float32 [1024, 1024], replicated, may hold values from -0.1875 to 0.1875
- neigh_bias: float32 [1024], replicated, may hold values from -3 to 3
- combine_proj: float32 [2048, 1024], replicated, may hold values from -0.125 to 0.125
- combine_bias: float32 [1024], replicated, may hold values from -3 to 3
- out_cot: float32 [2, 8192, 1024], P('grp', 'nodes'), as said below
Outputs:
- embedding: float32 [2, 8192, 1024], P('grp', 'nodes')
- penalty: float32 [], replicated
- grad_features: float32 [2, 8192, 1024], P('grp', 'nodes')
- grad_board_proj: float32 [1024, 1024], replicated
- grad_neigh_proj: float32 [1024, 1024], replicated
- grad_neigh_bias: float32 [1024], replicated
- grad_combine_proj: float32 [2048, 1024], replicated
- grad_combine_bias: float32 [1024], replicated
Inputs may be any that keep to these rules, and one draw needn't show every extreme that they name: `edge_slot`: each value occurs at least once among the 25600 edges of one device; value s sends to the device s // 128 of the same group. `out_cot`: entries are at most 192 / 16777216 in magnitude.
All inputs are finite; a program needn't handle non-finite values. No bound on the sum of `type_mask` on one device may be relied on, other than what follows from the above.
Results may differ from a plain program's by a relative error of at most 0.0069.
Values may be sent and summed in bfloat16 or wider, within the bound.
A program may use at most 128 MiB of HBM per device.

v0:
```python
import math

import jax
import jax.numpy as jnp
from jax import lax
from jax.sharding import PartitionSpec as P

HIGH = lax.Precision.HIGHEST


def gelu_tanh(v):
    return jax.nn.gelu(v, approximate=True)


def transposed(left, right):
    return lax.dot_general(
        left, right, (((0,), (0,)), ((), ())), preferred_element_type=jnp.float32
    )


def times_trans(left, right):
    return lax.dot_general(
        left, right, (((1,), (1,)), ((), ())), preferred_element_type=jnp.float32
    )


def build_spread(places, children, weights, slots, rows):
    edge_count = places.shape[0]
    block = math.gcd(edge_count, 1024)
    turns = edge_count // block
    slot_ids = jnp.arange(slots, dtype=jnp.int32)
    row_ids = jnp.arange(rows, dtype=jnp.int32)
    place_blocks = places.reshape(turns, block)
    child_blocks = children.reshape(turns, block)
    weight_blocks = weights.reshape(turns, block).astype(jnp.float32)

    def add_block(total, pieces):
        place, child, weight = pieces
        slot_hot = (place[:, None] == slot_ids[None, :]).astype(jnp.bfloat16)
        child_hot = jnp.where(child[:, None] == row_ids[None, :], weight[:, None], 0.0).astype(
            jnp.bfloat16
        )
        return (total + transposed(slot_hot, child_hot), None)

    spread, _ = lax.scan(
        add_block,
        jnp.zeros((slots, rows), jnp.float32),
        (place_blocks, child_blocks, weight_blocks),
    )
    return spread


def on_device(
    features,
    type_mask,
    edge_child,
    edge_slot,
    edge_weight,
    recv_rows,
    board_proj,
    neigh_proj,
    neigh_bias,
    combine_proj,
    combine_bias,
    out_cot,
):
    feats = features[0]
    board = (type_mask[0] == 1)[:, None]
    rows, width = feats.shape
    peers = recv_rows.shape[2]
    cap = recv_rows.shape[3]
    slots = peers * cap
    spread = build_spread(edge_slot[0], edge_child[0], edge_weight[0], slots, rows)
    totals = jnp.sum(spread, axis=1).astype(jnp.int32).reshape(peers, cap)
    arrived_tot = lax.all_to_all(totals, "nodes", split_axis=0, concat_axis=0, tiled=True)
    pbl = board_proj.astype(jnp.bfloat16)
    qwl = neigh_proj.astype(jnp.bfloat16)
    cwl = combine_proj.astype(jnp.bfloat16)
    featb = feats.astype(jnp.bfloat16)
    proj = jnp.dot(featb, pbl, preferred_element_type=jnp.float32)
    hidden = jnp.where(board, proj, feats).astype(jnp.bfloat16)
    pre = jnp.dot(hidden, qwl, preferred_element_type=jnp.float32) + neigh_bias
    message, gelu_msg = jax.vjp(gelu_tanh, pre)
    spread_b = spread.astype(jnp.bfloat16)
    slot_sums = jnp.dot(spread_b, message.astype(jnp.bfloat16), preferred_element_type=jnp.float32)
    slot_sums = slot_sums.astype(jnp.bfloat16).reshape(peers, cap, width)
    arrived = lax.all_to_all(slot_sums, "nodes", split_axis=0, concat_axis=0, tiled=True)
    targets = recv_rows[0, 0].reshape(-1)
    picker_bool = targets[None, :] == jnp.arange(rows, dtype=jnp.int32)[:, None]
    picker = picker_bool.astype(jnp.bfloat16)
    num = jnp.dot(picker, arrived.reshape(slots, width), preferred_element_type=jnp.float32)
    den = 1.0 + jnp.dot(
        picker_bool.astype(jnp.float32), arrived_tot.reshape(-1).astype(jnp.float32), precision=HIGH
    )
    aggb = (num / den[:, None]).astype(jnp.bfloat16)
    zpre = jnp.dot(hidden, cwl[:width], preferred_element_type=jnp.float32)
    zpre = zpre + jnp.dot(aggb, cwl[width:], preferred_element_type=jnp.float32) + combine_bias
    zval, gelu_z = jax.vjp(gelu_tanh, zpre)
    sumsq = jnp.sum(zval * zval, axis=1)
    inverse = lax.rsqrt(sumsq + 1e-06)
    embed = zval * inverse[:, None]
    board_count, board_sq = lax.psum(
        (jnp.sum(board.astype(jnp.float32)), jnp.sum(jnp.where(board[:, 0], sumsq, 0.0))),
        ("nodes", "grp"),
    )
    scale = 1.0 / (width * (1.0 + board_count))
    penalty = board_sq * scale
    cot = out_cot[0]
    dz = inverse[:, None] * (cot - embed * jnp.sum(cot * embed, axis=1, keepdims=True))
    dz = dz + jnp.where(board, 2.0 * scale * zval, 0.0)
    dzb = gelu_z(dz)[0].astype(jnp.bfloat16)
    joined = jnp.concatenate([hidden, aggb], axis=1)
    grad_comb = transposed(joined, dzb)
    grad_cbias = jnp.sum(dzb.astype(jnp.float32), axis=0)
    dcat = times_trans(dzb, cwl)
    dnum = (dcat[:, width:] / den[:, None]).astype(jnp.bfloat16)
    back_slots = transposed(picker, dnum).astype(jnp.bfloat16).reshape(peers, cap, width)
    returned = lax.all_to_all(back_slots, "nodes", split_axis=0, concat_axis=0, tiled=True)
    dmsg = transposed(spread_b, returned.reshape(slots, width))
    dpre = gelu_msg(dmsg)[0].astype(jnp.bfloat16)
    grad_qbias = jnp.sum(dpre.astype(jnp.float32), axis=0)
    grad_neigh = transposed(hidden, dpre)
    dhid = (dcat[:, :width] + times_trans(dpre, qwl)).astype(jnp.bfloat16)
    dproj = jnp.where(board, dhid, jnp.zeros_like(dhid))
    grad_board = transposed(featb, dproj)
    grad_feats = jnp.where(board, times_trans(dproj, pbl), dhid.astype(jnp.float32))
    grad_board, grad_neigh, grad_qbias, grad_comb, grad_cbias = lax.psum(
        (grad_board, grad_neigh, grad_qbias, grad_comb, grad_cbias), ("nodes", "grp")
    )
    return (
        embed[None],
        penalty,
        grad_feats[None],
        grad_board,
        grad_neigh,
        grad_qbias,
        grad_comb,
        grad_cbias,
    )


def solution(mesh):
    in_specs = (
        P("grp", "nodes", None),
        P("grp", "nodes"),
        P("grp", "nodes"),
        P("grp", "nodes"),
        P("grp", "nodes"),
        P("grp", "nodes", None, None),
        P(),
        P(),
        P(),
        P(),
        P(),
        P("grp", "nodes", None),
    )
    out_specs = (P("grp", "nodes", None), P(), P("grp", "nodes", None), P(), P(), P(), P(), P())
    return jax.shard_map(
        on_device, mesh=mesh, in_specs=in_specs, out_specs=out_specs, check_vma=False
    )
```

profile of v0, /device:TPU:0, one launch (start us, length us, event | category | flops | bytes accessed | tf_op | source)
XLA Modules:
  0.0 782.6 jit_solution(5996691668691222234)
XLA Ops:
  12.5 181.1 %while.11 = (s32[]{:T(128)}, f32[2048,512]{1,0:T(8,128)}, s32[25,1024]{1,0:T(8,128)S(1)}, s32[25,1024]{1,0:T(8,128)S(1)}, f32[25,1024]{1,0:T(8,128)S(1)}, /*index=5*/s32[]{:T(128)}, s32[]{:T(128)}) while((s32[]{:T(128)}, f32[2048,512]{1,0:T(8,128)}, s32[25,1024]{1,0:T(8,128)S(1)}, s32[25,1024]{1,0:T(8,128)S(1)}, ...), condition=%wide.region_1.2_spmd.clone, body=%wide.region_0.1_spmd.clone.sunk | while | flops 2152726528 | bytes 8425567 | solution.py:45
  25.1 7.3 select_add_fusion.2
  32.4 7.3 select_add_fusion.2
  47.0 7.3 select_add_fusion.2
  54.4 7.3 select_add_fusion.2
  69.0 7.3 select_add_fusion.2
  76.4 7.3 select_add_fusion.2
  91.0 7.3 select_add_fusion.2
  98.3 7.3 select_add_fusion.2
  113.0 7.3 select_add_fusion.2
  120.3 7.3 select_add_fusion.2
  135.0 7.3 select_add_fusion.2
  142.3 7.3 select_add_fusion.2
  157.0 7.3 select_add_fusion.2
  164.3 7.3 select_add_fusion.2
  179.0 7.3 select_add_fusion.2
  186.3 7.3 select_add_fusion.2
  196.9 7.4 all-to-all-start.1
  222.5 113.5 %psum.50 = f32[]{:T(128)} all-reduce(f32[]{:T(128)} %fusion.68), channel_id=1, replica_groups=mesh['nodes'=16,'grp'=2] {'nodes','grp'}, use_global_device_ids=true, to_apply=%region_7.8 | all-reduce | flops 1 | bytes 8 | tf_op jit(solution)/shard_map/psum | solution.py:102
  371.3 7.3 fusion.34
  378.6 70.1 %all-to-all-done.2 = bf16[16,128,1024]{2,1,0:T(8,128)(2,1)} async-done(((bf16[16,128,1024]{2,1,0:T(8,128)(2,1)}), bf16[16,128,1024]{2,1,0:T(8,128)(2,1)}, u32[]{:S(2)}, u32[]{:S(2)}) %all-to-all-start.2) | async-done | bytes 4194336 | tf_op jit(solution)/shard_map/all_to_all | solution.py:118
  448.7 7.8 convert_reduce_fusion.1
  464.6 57.2 %all-reduce = (f32[]{:T(128)}, f32[1024]{0:T(1024)}, f32[1024]{0:T(1024)}) all-reduce(f32[]{:T(128)} %get-tuple-element.97, f32[1024]{0:T(1024)S(1)} %get-tuple-element.101, f32[1024]{0:T(1024)S(1)} %get-tuple-element.92), channel_id=1, replica_groups=mesh['nodes'=16,'grp'=2] {'nodes','grp'}, use_global_device_ids=true, to_apply=%region_5.6 | all-reduce | flops 2049 | bytes 16392 | tf_op jit(solution)/shard_map/psum | solution.py:102
  527.4 232.4 %all-reduce.4.cloned.1.call-done = (f32[1024,1024]{0,1:T(8,128)}, f32[1024,1024]{1,0:T(8,128)}, f32[2048,1024]{1,0:T(8,128)}) async-done(((f32[1024,1024]{0,1:T(8,128)}, f32[1024,1024]{1,0:T(8,128)}, f32[2048,1024]{1,0:T(8,128)}), (f32[1024,1024]{0,1:T(8,128)}, f32[1024,1024]{1,0:T(8,128)}, f32[2048,1024]{1,0:T(8,128)})) %all-reduce.4.cloned.1.call-update) | async-done | bytes 16777232 | tf_op jit(solution)/shard_map/psum | solution.py:127
  (134 shorter events, 153.0 us)
Async XLA Ops:
  193.6 10.7 %copy-start.12 = (s32[1,512]{1,0:T(1,128)S(1)}, s32[1,512]{1,0:T(1,128)}, u32[]{:S(2)}) copy-start(s32[1,512]{1,0:T(1,128)} %param.15) | copy-start | bytes 6148
  193.6 10.7 %copy-start.2 = (f32[1,512,1024]{2,1,0:T(8,128)S(1)}, f32[1,512,1024]{2,1,0:T(8,128)}, u32[]{:S(2)}) copy-start(f32[1,512,1024]{2,1,0:T(8,128)} %param.14) | copy-start | bytes 6291460
  196.9 19.0 %all-to-all-start.1 = ((s32[16,1,128]{2,1,0:T(1,128)}), s32[16,1,128]{2,1,0:T(1,128)S(1)}, u32[]{:S(2)}, u32[]{:S(2)}) async-start(s32[16,1,128]{2,1,0:T(1,128)} %bitcast.4), calls=%async_computation.1 | async-start | bytes 16384 | tf_op jit(solution)/shard_map/all_to_all | solution.py:75
  204.3 3.6 copy-start.6
  208.0 163.4 %copy-start.3 = (bf16[512,1024]{1,0:T(8,128)(2,1)}, bf16[512,1024]{1,0:T(8,128)(2,1)S(1)}, u32[]{:S(2)}) copy-start(bf16[512,1024]{1,0:T(8,128)(2,1)S(1)} %fusion.41) | copy-start | bytes 3145732
  208.0 3.3 copy-start.8
  208.0 3.3 copy-start.15
  209.3 1.3 copy-start.17
  215.9 128.9 %all-to-all-start = ((bf16[16,128,1024]{2,1,0:T(8,128)(2,1)}), bf16[16,128,1024]{2,1,0:T(8,128)(2,1)}, u32[]{:S(2)}, u32[]{:S(2)}) async-start(bf16[16,128,1024]{2,1,0:T(8,128)(2,1)} %bitcast.66), calls=%async_computation | async-start | bytes 8388608 | tf_op jit(solution)/shard_map/all_to_all | solution.py:87
  336.1 6.8 copy-start.13
  344.8 5.7 copy-start.5
  349.5 1.0 copy-start.16
  350.5 1.3 copy-start.14
  351.7 2.5 copy-start
  358.5 2.4 copy-start.9
  360.9 4.5 copy-start.10
  365.4 83.3 %all-to-all-start.2 = ((bf16[16,128,1024]{2,1,0:T(8,128)(2,1)}), bf16[16,128,1024]{2,1,0:T(8,128)(2,1)}, u32[]{:S(2)}, u32[]{:S(2)}) async-start(bf16[16,128,1024]{2,1,0:T(8,128)(2,1)} %bitcast.67), calls=%async_computation.2 | async-start | bytes 8388608 | tf_op jit(solution)/shard_map/all_to_all | solution.py:118
  371.1 388.7 %all-reduce.4.cloned.1.call-start = ((), (), s32[]{:S(2)}) async-start(), calls=%async_computation.3 | async-start | bytes 33554432 | tf_op jit(solution)/shard_map/psum | solution.py:127
  448.7 7.8 copy-start.7
  448.7 7.8 copy-start.11
  456.5 1.3 copy-start.4
  765.1 6.2 copy-start.1
Sparse Core Ops, SparseCore 0:
  464.7 294.9 all-reduce.3
where the time goes:
time: 784 us; the launch traced here: 783 us
  waiting for transfers between devices  302 us (39%)
  matrix products  234 us (30%)
  blocking collectives  171 us (22%)
  other arithmetic  19.7 us (3%)
  starting transfers between devices  19.4 us (2%)
  local copies, waits for them, and re-layouts  19.1 us (2%)
  between operations  16.8 us (2%)
    psum x1, waiting for transfers between devices, on_device(): lax.psum((grad_board, grad_neigh, grad_qbias, grad_comb, grad_cbias), ('n...  232 us
    dot_general x30, matrix products, transposed(): lax.dot_general(left, right, (((0,), (0,)), ((), ())), preferred_element_...  206 us
    psum x2, blocking collectives, on_device(): lax.psum((jnp.sum(board.astype(jnp.float32)), jnp.sum(jnp.where(board[:,...  171 us
    all_to_all x1, waiting for transfers between devices, on_device(): lax.all_to_all(back_slots, 'nodes', split_axis=0, concat_axis=0, tiled=True)  70.1 us
    unnamed x40, local copies, waits for them, and re-layouts  18.4 us
  transfers between devices with their start and end apart: 4, of which 2 were waited for; matrix products, arithmetic and copies ran while one was open for 4% of the time, Pallas kernels for 0%

commit v1 on v0

v1 whole, which is shorter than its diff:
```python
import functools

import jax
import jax.numpy as jnp
from jax import lax
from jax.experimental import pallas as pl
from jax.experimental.pallas import tpu as pltpu
from jax.sharding import PartitionSpec as P

HIGH = lax.Precision.HIGHEST
MESH = pl.DeviceIdType.MESH
BF16 = jnp.bfloat16
F32 = jnp.float32
F8 = jnp.float8_e4m3fn
MIB = 2**20


def gelu_tanh(v):
    return jax.nn.gelu(v, approximate=True)


def dot_nt(left, right):
    return lax.dot_general(
        left, right, (((1,), (1,)), ((), ())), preferred_element_type=F32
    )


def dot_tn(left, right):
    return lax.dot_general(
        left, right, (((0,), (0,)), ((), ())), preferred_element_type=F32
    )


def spread_kernel(turn, slot_ref, child_ref, weight_ref, out_ref):
    slots, rows = out_ref.shape
    edges = slot_ref.shape[1]
    block = 256
    out_ref[...] = jnp.zeros_like(out_ref)

    @pl.loop(0, edges // turn)
    def _(i):
        at = pl.ds(pl.multiple_of(i * turn, turn), turn)
        slot = slot_ref[:, at].astype(jnp.int16)
        child = child_ref[:, at].astype(jnp.int16)
        weight = weight_ref[:, at].astype(F32).astype(F8)
        right = jnp.where(
            lax.broadcasted_iota(jnp.int16, (rows, turn), 0) == child, weight, jnp.zeros((), F8)
        )
        for first in range(0, slots, block):
            ids = lax.broadcasted_iota(jnp.int16, (block, turn), 0) + jnp.asarray(first, jnp.int16)
            left = jnp.where(ids == slot, jnp.ones((), F8), jnp.zeros((), F8))
            out_ref[pl.ds(first, block), :] += dot_nt(left, right)


def build_spread(place, child, weight, slots, rows):
    edges = place.shape[0]
    return pl.pallas_call(
        functools.partial(spread_kernel, 1024),
        out_shape=jax.ShapeDtypeStruct((slots, rows), F32),
        in_specs=[pl.BlockSpec(memory_space=pltpu.VMEM)] * 3,
        out_specs=pl.BlockSpec(memory_space=pltpu.VMEM),
        compiler_params=pltpu.CompilerParams(vmem_limit_bytes=32 * MIB),
        cost_estimate=pl.CostEstimate(
            flops=2 * edges * slots * rows, bytes_accessed=4 * slots * rows, transcendentals=0
        ),
        name="build_spread",
    )(place.reshape(1, edges), child.reshape(1, edges), weight.reshape(1, edges))


class Place:
    def __init__(self, n_nodes, n_grp):
        node = lax.axis_index("nodes")
        grp = lax.axis_index("grp")
        self.node, self.grp = node, grp
        self.size = {"c": 2, "y": 2, "z": n_nodes // 4, "x": n_grp}
        self.at = {
            "c": lax.rem(node, 2),
            "y": lax.rem(node // 2, 2),
            "z": node // 4,
            "x": grp,
        }

    def member(self, axis, index):
        at = dict(self.at)
        at[axis] = index
        return {"nodes": at["z"] * 4 + at["y"] * 2 + at["c"], "grp": at["x"]}

    def others(self, axis):
        size = self.size[axis]
        for far in range(1, size):
            index = lax.rem(self.at[axis] + far, size)
            yield far - 1, index, self.member(axis, index)


def barrier(place, axes):
    sem = pltpu.get_barrier_semaphore()
    count = 0
    for axis in axes:
        for _, _, device in place.others(axis):
            pl.semaphore_signal(sem, inc=1, device_id=device, device_id_type=MESH)
            count += 1
    pl.semaphore_wait(sem, count)


def add_into(target, first, count, columns, parts, step=16):
    @pl.loop(0, count // step)
    def _(i):
        at = pl.ds(pl.multiple_of(first + i * step, step), step)
        total = target[at, columns].astype(F32)
        for part in parts:
            total += part[pl.ds(pl.multiple_of(i * step, step), step), :].astype(F32)
        target[at, columns] = total.astype(target.dtype)


def reduce_job(place, order, first, rows, grad, out, arrive, land, send, recv, base):
    half = grad.shape[1] // 2
    core = place.at["c"]
    mine = pl.ds(pl.multiple_of(core * half, half), half)
    theirs = pl.ds(pl.multiple_of((1 - core) * half, half), half)
    sem = base
    mate = place.member("c", 1 - core)
    block = pl.ds(first, rows)
    copy = pltpu.make_async_remote_copy(
        src_ref=grad.at[block, theirs],
        dst_ref=arrive,
        send_sem=send.at[sem],
        recv_sem=recv.at[sem],
        device_id=mate,
        device_id_type=MESH,
    )
    copy.start()
    sem += 1
    yield
    copy.wait()
    add_into(grad, first, rows, mine, [arrive])
    begin, length, used = first, rows, 0
    trail = []
    for axis in order:
        size = place.size[axis]
        length //= size
        copies, parts = [], []
        for far, index, device in place.others(axis):
            start = pl.multiple_of(begin + index * length, 16)
            slot = land.at[pl.ds(used, length)]
            used += length
            copy = pltpu.make_async_remote_copy(
                src_ref=grad.at[pl.ds(start, length), mine],
                dst_ref=slot,
                send_sem=send.at[sem],
                recv_sem=recv.at[sem],
                device_id=device,
                device_id_type=MESH,
            )
            copy.start()
            sem += 1
            copies.append(copy)
            parts.append(slot)
        yield
        for copy in copies:
            copy.wait()
        trail.append((axis, begin, length))
        begin = pl.multiple_of(begin + place.at[axis] * length, 16)
        add_into(grad, begin, length, mine, parts)
    at = pl.ds(begin, length)
    out[at, mine] = grad[at, mine]
    for axis, parent, piece in reversed(trail):
        size = place.size[axis]
        start = pl.multiple_of(parent + place.at[axis] * piece, 16)
        own = out.at[pl.ds(start, piece), mine]
        copies = []
        for far, index, device in place.others(axis):
            copy = pltpu.make_async_remote_copy(
                src_ref=own,
                dst_ref=own,
                send_sem=send.at[sem],
                recv_sem=recv.at[sem],
                device_id=device,
                device_id_type=MESH,
            )
            copy.start()
            sem += 1
            copies.append(copy)
        yield
        for copy in copies:
            copy.wait()
    own = out.at[block, mine]
    copy = pltpu.make_async_remote_copy(
        src_ref=own,
        dst_ref=own,
        send_sem=send.at[sem],
        recv_sem=recv.at[sem],
        device_id=mate,
        device_id_type=MESH,
    )
    copy.start()
    yield
    copy.wait()


def job_sems(n_nodes, n_grp):
    return 2 * (1 + (2 - 1) + (n_nodes // 4 - 1) + (n_grp - 1))


def run_jobs(jobs, at_once):
    waiting, running = list(jobs), []
    while waiting or running:
        left = []
        for job in running:
            try:
                next(job)
                left.append(job)
            except StopIteration:
                pass
        for job in waiting[:at_once]:
            next(job)
            left.append(job)
        waiting = waiting[at_once:]
        running = left


def reduce_kernel(n_nodes, n_grp, count, grad_hbm, out_hbm, grad, out, arrive, land, send, recv, sem_in, sem_out):
    place = Place(n_nodes, n_grp)
    rows = grad.shape[0] // count
    loads = []
    for j in range(count):
        at = pl.ds(j * rows, rows)
        load = pltpu.make_async_copy(grad_hbm.at[at], grad.at[at], sem_in.at[j])
        load.start()
        loads.append(load)
    barrier(place, ("c", "x", "y", "z"))
    per_job = job_sems(n_nodes, n_grp)

    def job(j):
        at = pl.ds(j * rows, rows)
        loads[j].wait()
        yield from reduce_job(
            place,
            ("x", "y", "z") if j % 2 == 0 else ("y", "x", "z"),
            j * rows,
            rows,
            grad,
            out,
            arrive.at[at],
            land.at[pl.ds(j * 2 * rows, 2 * rows)],
            send,
            recv,
            j * per_job,
        )
        store = pltpu.make_async_copy(out.at[at], out_hbm.at[at], sem_out.at[j])
        store.start()
        stores.append(store)

    stores = []
    run_jobs([job(j) for j in range(count)], 2)
    for store in stores:
        store.wait()


def all_reduce(grads, n_nodes, n_grp):
    rows, width = grads.shape
    count = max(1, min(8, rows * 2 // (16 * n_nodes * n_grp)))
    sems = count * job_sems(n_nodes, n_grp)
    return pl.pallas_call(
        functools.partial(reduce_kernel, n_nodes, n_grp, count),
        out_shape=jax.ShapeDtypeStruct((rows, width), BF16),
        in_specs=[pl.BlockSpec(memory_space=pl.ANY)],
        out_specs=pl.BlockSpec(memory_space=pl.ANY),
        scratch_shapes=[
            pltpu.VMEM((rows, width), BF16),
            pltpu.VMEM((rows, width), BF16),
            pltpu.VMEM((rows, width // 2), BF16),
            pltpu.VMEM((2 * rows, width // 2), BF16),
            pltpu.SemaphoreType.DMA((sems,)),
            pltpu.SemaphoreType.DMA((sems,)),
            pltpu.SemaphoreType.DMA((count,)),
            pltpu.SemaphoreType.DMA((count,)),
        ],
        compiler_params=pltpu.CompilerParams(
            vmem_limit_bytes=48 * MIB, collective_id=1, has_side_effects=True
        ),
        name="sum_gradients",
    )(grads)


def on_device(
    n_nodes,
    n_grp,
    features,
    type_mask,
    edge_child,
    edge_slot,
    edge_weight,
    recv_rows,
    board_proj,
    neigh_proj,
    neigh_bias,
    combine_proj,
    combine_bias,
    out_cot,
):
    feats = features[0]
    board = (type_mask[0] == 1)[:, None]
    rows, width = feats.shape
    peers = recv_rows.shape[2]
    cap = recv_rows.shape[3]
    slots = peers * cap
    board_count = lax.psum(jnp.sum(type_mask[0]).astype(F32), ("nodes", "grp"))
    scale = 1.0 / (width * (1.0 + board_count))
    spread = build_spread(edge_slot[0], edge_child[0], edge_weight[0], slots, rows)
    totals = jnp.sum(spread, axis=1).astype(jnp.int32).reshape(peers, cap)
    arrived_tot = lax.all_to_all(totals, "nodes", split_axis=0, concat_axis=0, tiled=True)
    pbl = board_proj.astype(BF16)
    qwl = neigh_proj.astype(BF16)
    cwl = combine_proj.astype(BF16)
    featb = feats.astype(BF16)
    proj = jnp.dot(featb, pbl, preferred_element_type=F32)
    hidden = jnp.where(board, proj, feats).astype(BF16)
    pre = jnp.dot(hidden, qwl, preferred_element_type=F32) + neigh_bias
    message, gelu_msg = jax.vjp(gelu_tanh, pre)
    spread_b = spread.astype(BF16)
    slot_sums = jnp.dot(spread_b, message.astype(BF16), preferred_element_type=F32)
    slot_sums = slot_sums.astype(BF16).reshape(peers, cap, width)
    arrived = lax.all_to_all(slot_sums, "nodes", split_axis=0, concat_axis=0, tiled=True)
    targets = recv_rows[0, 0].reshape(-1)
    picker_bool = targets[None, :] == jnp.arange(rows, dtype=jnp.int32)[:, None]
    picker = picker_bool.astype(BF16)
    num = jnp.dot(picker, arrived.reshape(slots, width), preferred_element_type=F32)
    den = 1.0 + jnp.dot(
        picker_bool.astype(F32), arrived_tot.reshape(-1).astype(F32), precision=HIGH
    )
    aggb = (num / den[:, None]).astype(BF16)
    zpre = jnp.dot(hidden, cwl[:width], preferred_element_type=F32)
    zpre = zpre + jnp.dot(aggb, cwl[width:], preferred_element_type=F32) + combine_bias
    zval, gelu_z = jax.vjp(gelu_tanh, zpre)
    sumsq = jnp.sum(zval * zval, axis=1)
    inverse = lax.rsqrt(sumsq + 1e-06)
    embed = zval * inverse[:, None]
    board_sq = jnp.sum(jnp.where(board[:, 0], sumsq, 0.0))
    cot = out_cot[0]
    dz = inverse[:, None] * (cot - embed * jnp.sum(cot * embed, axis=1, keepdims=True))
    dz = dz + jnp.where(board, 2.0 * scale * zval, 0.0)
    dzb = gelu_z(dz)[0].astype(BF16)
    joined = jnp.concatenate([hidden, aggb], axis=1)
    grad_comb = dot_tn(joined, dzb).astype(BF16)
    grad_cbias = jnp.sum(dzb.astype(F32), axis=0)
    dcat = dot_nt(dzb, cwl)
    dnum = (dcat[:, width:] / den[:, None]).astype(BF16)
    back_slots = dot_tn(picker, dnum).astype(BF16).reshape(peers, cap, width)
    returned = lax.all_to_all(back_slots, "nodes", split_axis=0, concat_axis=0, tiled=True)
    dmsg = dot_tn(spread_b, returned.reshape(slots, width))
    dpre = gelu_msg(dmsg)[0].astype(BF16)
    grad_qbias = jnp.sum(dpre.astype(F32), axis=0)
    grad_neigh = dot_tn(hidden, dpre).astype(BF16)
    dhid = (dcat[:, :width] + dot_nt(dpre, qwl)).astype(BF16)
    dproj = jnp.where(board, dhid, jnp.zeros_like(dhid))
    grad_board = dot_tn(featb, dproj).astype(BF16)
    grad_feats = jnp.where(board, dot_nt(dproj, pbl), dhid.astype(F32))
    small = lax.psum(
        jnp.concatenate([grad_qbias, grad_cbias, jnp.full((width,), board_sq)]), ("nodes", "grp")
    )
    penalty = small[2 * width] * scale
    summed = all_reduce(
        jnp.concatenate([grad_comb, grad_neigh, grad_board], axis=0), n_nodes, n_grp
    )
    return (
        embed[None],
        penalty,
        grad_feats[None],
        summed[3 * width :].astype(F32),
        summed[2 * width : 3 * width].astype(F32),
        small[:width],
        summed[: 2 * width].astype(F32),
        small[width : 2 * width],
    )


def solution(mesh):
    in_specs = (
        P("grp", "nodes", None),
        P("grp", "nodes"),
        P("grp", "nodes"),
        P("grp", "nodes"),
        P("grp", "nodes"),
        P("grp", "nodes", None, None),
        P(),
        P(),
        P(),
        P(),
        P(),
        P("grp", "nodes", None),
    )
    out_specs = (P("grp", "nodes", None), P(), P("grp", "nodes", None), P(), P(), P(), P(), P())
    return jax.shard_map(
        functools.partial(on_device, mesh.shape["nodes"], mesh.shape["grp"]),
        mesh=mesh,
        in_specs=in_specs,
        out_specs=out_specs,
        check_vma=False,
    )
```

time: 784 us -> 465 us (0.59)
  waiting for transfers between devices: 302 us -> 71.8 us
  matrix products: 234 us -> 46.2 us
  Pallas kernels: 0 us -> 132 us
  blocking collectives: 171 us -> 152 us
  between operations: 16.8 us -> 4.1 us
  other arithmetic: 19.7 us -> 30.1 us
  local copies, waits for them, and re-layouts: 19.1 us -> 9.35 us
    psum x1 -> x0, waiting for transfers between devices: 232 us -> none  [on_device(): lax.psum((grad_board, grad_neigh, grad_qbias, grad_comb, grad_cbias), ('n...]
    dot_general x40 -> x15, matrix products: 234 us -> 46.2 us  [the longest x5 20.8 us: dot_tn(): lax.dot_general(left, right, (((0,), (0,)), ((), ())), preferred_element_...]
    pallas_call x0 -> x2, Pallas kernels: none -> 132 us  [the longest x1 100 us: all_reduce(): pl.pallas_call(functools.partial(reduce_kernel, n_nodes, n_grp, count), o...]
    psum x2, blocking collectives: 171 us -> 152 us  [the longest x1 113 us: on_device(): board_count = lax.psum(jnp.sum(type_mask[0]).astype(F32), ('nodes', 'grp'))]
    unnamed x40 -> x46, local copies, waits for them, and re-layouts: 18.4 us -> 7.59 us
    convert_element_type x2 -> x3, other arithmetic: 7.26 us -> 17.3 us  [the longest x1 6.83 us: on_device(): summed[2 * width:3 * width].astype(F32)]
  transfers between devices with their start and end apart: 4 -> 3, of which waited for: 2 -> 1; matrix products, arithmetic and copies ran while one was open for 4% -> 5% of each run, Pallas kernels for 0% -> 0%
where the time goes in v1:
time: 465 us; the launch traced here: 464 us
  blocking collectives  152 us (33%)
  Pallas kernels  132 us (28%)
  waiting for transfers between devices  71.8 us (15%)
  matrix products  46.2 us (10%)
  other arithmetic  30.1 us (6%)
  starting transfers between devices  19.1 us (4%)
  local copies, waits for them, and re-layouts  9.35 us (2%)
    psum x1, blocking collectives, on_device(): board_count = lax.psum(jnp.sum(type_mask[0]).astype(F32), ('nodes', 'grp'))  113 us
    pallas_call x1, Pallas kernels, all_reduce(): pl.pallas_call(functools.partial(reduce_kernel, n_nodes, n_grp, count), o...  100 us
    all_to_all x1, waiting for transfers between devices, on_device(): lax.all_to_all(back_slots, 'nodes', split_axis=0, concat_axis=0, tiled=True)  71.8 us
    psum x1, blocking collectives, on_device(): lax.psum(jnp.concatenate([grad_qbias, grad_cbias, jnp.full((width,), boar...  38.6 us
    pallas_call x1, Pallas kernels, build_spread(): pl.pallas_call(functools.partial(spread_kernel, 1024), out_shape=jax.Shap...  31.5 us
    dot_general x5, matrix products, dot_tn(): lax.dot_general(left, right, (((0,), (0,)), ((), ())), preferred_element_...  20.8 us
  transfers between devices with their start and end apart: 3, of which 1 were waited for; matrix products, arithmetic and copies ran while one was open for 5% of the time, Pallas kernels for 0%

profile of v1, /device:TPU:0, one launch (start us, length us, event | category | flops | bytes accessed | tf_op | source)
XLA Modules:
  0.0 463.9 jit_solution(14280054402599875401)
XLA Ops:
  3.3 31.5 %build_spread.1 = f32[2048,512]{1,0:T(8,128)S(1)} custom-call(s32[1,25600]{1,0:T(1,128)S(1)} %copy-done.2, s32[1,25600]{1,0:T(1,128)S(1)} %copy-done.3, s32[1,25600]{1,0:T(1,128)S(1)} %copy-done.4), custom_call_target="tpu_custom_call" | custom-call | flops 53687091200 | bytes 4194304 | tf_op jit(solution)/shard_map/build_spread/pallas_call | solution.py:57
  34.8 2.0 copy-done
  36.9 2.7 reduce_sum.63
  40.1 7.4 %all-to-all-start.1 = ((s32[16,1,128]{2,1,0:T(1,128)}), s32[16,1,128]{2,1,0:T(1,128)S(1)}, u32[]{:S(2)}, u32[]{:S(2)}) async-start(s32[16,1,128]{2,1,0:T(1,128)} %bitcast.4), calls=%async_computation.1 | async-start | bytes 16384 | tf_op jit(solution)/shard_map/all_to_all | solution.py:311
  47.6 3.6 fusion.30
  54.5 4.6 convolution_convert_fusion.1
  59.1 6.1 %all-to-all-start = ((bf16[16,128,1024]{2,1,0:T(8,128)(2,1)}), bf16[16,128,1024]{2,1,0:T(8,128)(2,1)}, u32[]{:S(2)}, u32[]{:S(2)}) async-start(bf16[16,128,1024]{2,1,0:T(8,128)(2,1)} %bitcast.58), calls=%async_computation | async-start | bytes 8388608 | tf_op jit(solution)/shard_map/all_to_all | solution.py:323
  66.5 112.9 %psum.14 = f32[]{:T(128)} all-reduce(f32[]{:T(128)S(6)} %convert_element_type.110), channel_id=1, replica_groups=mesh['nodes'=16,'grp'=2] {'nodes','grp'}, use_global_device_ids=true, to_apply=%region_4.5 | all-reduce | flops 1 | bytes 8 | tf_op jit(solution)/shard_map/psum | solution.py:307
  179.4 6.1 %convert_element_type.100 = bf16[2048,1024]{1,0:T(8,128)(2,1)} convert(f32[2048,1024]{1,0:T(8,128)} %param.21) | non-fusion elementwise | flops 2097152 | bytes 12582912 | tf_op jit(solution)/shard_map/convert_element_type | solution.py:314
  186.2 1.9 fusion.1
  188.1 4.7 %divide_convert_fusion = bf16[512,1024]{1,0:T(8,128)(2,1)S(1)} fusion(bf16[2048,1024]{1,0:T(8,128)(2,1)} %bitcast.3, s32[2048]{0:T(1024)S(1)} %bitcast.62, f32[512]{0:T(512)S(1)} %broadcast_add_fusion), kind=kOutput, calls=%fused_computation.54 | convolution fusion | flops 2149580800 | bytes 5253120 | tf_op jit(solution)/shard_map/dot_general | solution.py:327
  197.5 3.4 convert_reduce_fusion
  200.9 2.4 fusion.69
  203.3 4.5 fusion.3
  207.8 5.7 %all-to-all-start.2 = ((bf16[16,128,1024]{2,1,0:T(8,128)(2,1)}), bf16[16,128,1024]{2,1,0:T(8,128)(2,1)}, u32[]{:S(2)}, u32[]{:S(2)}) async-start(bf16[16,128,1024]{2,1,0:T(8,128)(2,1)} %bitcast.59), calls=%async_computation.2 | async-start | bytes 8388608 | tf_op jit(solution)/shard_map/all_to_all | solution.py:349
  213.4 5.9 %convolution_convert_fusion = bf16[2048,1024]{1,0:T(8,128)(2,1)} fusion(bf16[512,1024]{1,0:T(8,128)(2,1)S(1)} %get-tuple-element.9, bf16[512,1024]{1,0:T(8,128)(2,1)} %copy-done.22, bf16[512,1024]{1,0:T(8,128)(2,1)} %copy-done.15), kind=kOutput, calls=%fused_computation.7 | convolution fusion | flops 2153775104 | bytes 7340032 | tf_op jit(solution)/shard_map/dot_general | solution.py:29
  219.3 71.8 %all-to-all-done.2 = bf16[16,128,1024]{2,1,0:T(8,128)(2,1)} async-done(((bf16[16,128,1024]{2,1,0:T(8,128)(2,1)}), bf16[16,128,1024]{2,1,0:T(8,128)(2,1)}, u32[]{:S(2)}, u32[]{:S(2)}) %all-to-all-start.2) | async-done | bytes 4194336 | tf_op jit(solution)/shard_map/all_to_all | solution.py:349
  291.1 7.8 %convert_reduce_fusion.1 = (f32[1024]{0:T(1024)S(1)}, bf16[512,1024]{1,0:T(8,128)(2,1)S(1)}) fusion(f32[512,1024]{1,0:T(8,128)} %copy-done.21, f32[1024]{0:T(1024)S(1)} %copy-done.20, bf16[2048,1024]{1,0:T(8,128)(2,1)} %bitcast.11, f32[2048,512]{1,0:T(8,128)} %copy-done), kind=kOutput, calls=%fused_computation.51 | convolution fusion | flops 2160589824 | bytes 11542528 | tf_op jit(solution)/shard_map/dot_general | solution.py:29
  303.7 3.9 pad_maximum_fusion.grad_hbm
  307.6 100.1 %sum_gradients.1 = bf16[4096,1024]{1,0:T(8,128)(2,1)} custom-call(bf16[4096,1024]{1,0:T(8,128)(2,1)} %pad_maximum_fusion.grad_hbm), custom_call_target="tpu_custom_call" | custom-call | tf_op jit(solution)/shard_map/sum_gradients/pallas_call | solution.py:263
  407.8 6.8 %slice_convert_fusion.1 = (f32[1024,1024]{1,0:T(8,128)}, f32[1024,1024]{1,0:T(8,128)}) fusion(bf16[4096,1024]{1,0:T(8,128)(2,1)} %sum_gradients.1), kind=kLoop, calls=%fused_computation.46 | loop fusion | flops 2097152 | bytes 12582912 | tf_op jit(solution)/shard_map/convert_element_type | solution.py:370
  414.6 4.4 slice_convert_fusion
  419.1 2.6 select_bitcast_fusion
  422.4 38.6 %psum.15 = f32[3072]{0:T(1024)S(1)} all-reduce(f32[3072]{0:T(1024)S(1)} %pad_maximum_fusion.1), channel_id=1, replica_groups=mesh['nodes'=16,'grp'=2] {'nodes','grp'}, use_global_device_ids=true, to_apply=%region_8.9 | all-reduce | flops 3072 | bytes 24576 | tf_op jit(solution)/shard_map/psum | solution.py:358
  (63 shorter events, 18.5 us)
Async XLA Ops:
  0.6 0.9 copy-start.2
  34.8 2.0 copy-start
  36.8 10.7 %copy-start.17 = (s32[1,512]{1,0:T(1,128)S(1)}, s32[1,512]{1,0:T(1,128)}, u32[]{:S(2)}) copy-start(s32[1,512]{1,0:T(1,128)} %param.13) | copy-start | bytes 6148
  36.8 10.7 %copy-start.12 = (f32[1,512,1024]{2,1,0:T(8,128)S(1)}, f32[1,512,1024]{2,1,0:T(8,128)}, u32[]{:S(2)}) copy-start(f32[1,512,1024]{2,1,0:T(8,128)} %param.12) | copy-start | bytes 6291460
  40.1 19.0 %all-to-all-start.1 = ((s32[16,1,128]{2,1,0:T(1,128)}), s32[16,1,128]{2,1,0:T(1,128)S(1)}, u32[]{:S(2)}, u32[]{:S(2)}) async-start(s32[16,1,128]{2,1,0:T(1,128)} %bitcast.4), calls=%async_computation.1 | async-start | bytes 16384 | tf_op jit(solution)/shard_map/all_to_all | solution.py:311
  47.6 3.6 copy-start.9
  51.2 142.9 %copy-start.15 = (bf16[512,1024]{1,0:T(8,128)(2,1)}, bf16[512,1024]{1,0:T(8,128)(2,1)S(1)}, u32[]{:S(2)}) copy-start(bf16[512,1024]{1,0:T(8,128)(2,1)S(1)} %fusion.30) | copy-start | bytes 3145732
  51.2 3.3 copy-start.1
  51.2 3.3 copy-start.20
  52.5 1.3 copy-start.21
  59.1 129.0 %all-to-all-start = ((bf16[16,128,1024]{2,1,0:T(8,128)(2,1)}), bf16[16,128,1024]{2,1,0:T(8,128)(2,1)}, u32[]{:S(2)}, u32[]{:S(2)}) async-start(bf16[16,128,1024]{2,1,0:T(8,128)(2,1)} %bitcast.58), calls=%async_computation | async-start | bytes 8388608 | tf_op jit(solution)/shard_map/all_to_all | solution.py:323
  179.4 6.8 %copy-start.18 = (s32[1,1,16,128]{3,2,1,0:T(8,128)S(1)}, s32[1,1,16,128]{3,2,1,0:T(8,128)}, u32[]{:S(2)}) copy-start(s32[1,1,16,128]{3,2,1,0:T(8,128)} %param.17) | copy-start | bytes 24580
  188.1 4.7 %copy-start.8 = (bf16[2048,1024]{1,0:T(8,128)(2,1)S(1)}, bf16[2048,1024]{1,0:T(8,128)(2,1)}, u32[]{:S(2)}) copy-start(bf16[2048,1024]{1,0:T(8,128)(2,1)} %convert_element_type.100) | copy-start | bytes 12582916
  192.8 1.3 copy-start.22
  192.8 1.3 copy-start.19
  194.1 2.5 copy-start.7
  203.3 4.5 copy-start.13
  207.8 83.3 %all-to-all-start.2 = ((bf16[16,128,1024]{2,1,0:T(8,128)(2,1)}), bf16[16,128,1024]{2,1,0:T(8,128)(2,1)}, u32[]{:S(2)}, u32[]{:S(2)}) async-start(bf16[16,128,1024]{2,1,0:T(8,128)(2,1)} %bitcast.59), calls=%async_computation.2 | async-start | bytes 8388608 | tf_op jit(solution)/shard_map/all_to_all | solution.py:349
  291.1 7.8 %copy-start.10 = (f32[1024,1024]{1,0:T(8,128)S(1)}, f32[1024,1024]{1,0:T(8,128)}, u32[]{:S(2)}) copy-start(f32[1024,1024]{1,0:T(8,128)} %param.19) | copy-start | bytes 12582916
  291.1 7.8 %copy-start.14 = (f32[512,2048]{1,0:T(8,128)S(1)}, f32[512,2048]{1,0:T(8,128)}, u32[]{:S(2)}) copy-start(f32[512,2048]{1,0:T(8,128)} %copy-done.13) | copy-start | bytes 12582916
  298.9 1.3 copy-start.16
  301.5 2.2 copy-start.11
  407.8 6.8 %copy-start.5 = (bf16[4096,1024]{1,0:T(8,128)(2,1)S(1)}, bf16[4096,1024]{1,0:T(8,128)(2,1)}, u32[]{:S(2)}) copy-start(bf16[4096,1024]{1,0:T(8,128)(2,1)} %sum_gradients.1) | copy-start | bytes 25165828
  414.6 4.4 copy-start.6
  (2 other events, 1.8 us)

commit v2 on v1

--- a/solution.py
+++ b/solution.py
@@ -1,4 +1,5 @@
 import functools
+import math
 
 import jax
 import jax.numpy as jnp
@@ -31,65 +32,46 @@
     )
 
 
-def spread_kernel(turn, slot_ref, child_ref, weight_ref, out_ref):
-    slots, rows = out_ref.shape
-    edges = slot_ref.shape[1]
-    block = 256
-    out_ref[...] = jnp.zeros_like(out_ref)
-
-    @pl.loop(0, edges // turn)
-    def _(i):
-        at = pl.ds(pl.multiple_of(i * turn, turn), turn)
-        slot = slot_ref[:, at].astype(jnp.int16)
-        child = child_ref[:, at].astype(jnp.int16)
-        weight = weight_ref[:, at].astype(F32).astype(F8)
-        right = jnp.where(
-            lax.broadcasted_iota(jnp.int16, (rows, turn), 0) == child, weight, jnp.zeros((), F8)
-        )
-        for first in range(0, slots, block):
-            ids = lax.broadcasted_iota(jnp.int16, (block, turn), 0) + jnp.asarray(first, jnp.int16)
-            left = jnp.where(ids == slot, jnp.ones((), F8), jnp.zeros((), F8))
-            out_ref[pl.ds(first, block), :] += dot_nt(left, right)
-
-
-def build_spread(place, child, weight, slots, rows):
-    edges = place.shape[0]
-    return pl.pallas_call(
-        functools.partial(spread_kernel, 1024),
-        out_shape=jax.ShapeDtypeStruct((slots, rows), F32),
-        in_specs=[pl.BlockSpec(memory_space=pltpu.VMEM)] * 3,
-        out_specs=pl.BlockSpec(memory_space=pltpu.VMEM),
-        compiler_params=pltpu.CompilerParams(vmem_limit_bytes=32 * MIB),
-        cost_estimate=pl.CostEstimate(
-            flops=2 * edges * slots * rows, bytes_accessed=4 * slots * rows, transcendentals=0
-        ),
-        name="build_spread",
-    )(place.reshape(1, edges), child.reshape(1, edges), weight.reshape(1, edges))
+LINE = 4
+CHUNKS = 4
 
 
 class Place:
     def __init__(self, n_nodes, n_grp):
+        layer = n_nodes // LINE
         node = lax.axis_index("nodes")
         grp = lax.axis_index("grp")
         self.node, self.grp = node, grp
-        self.size = {"c": 2, "y": 2, "z": n_nodes // 4, "x": n_grp}
-        self.at = {
-            "c": lax.rem(node, 2),
-            "y": lax.rem(node // 2, 2),
-            "z": node // 4,
-            "x": grp,
-        }
+        self.size = {"l": layer, "c": 2, "y": layer // 2, "z": LINE, "x": n_grp}
+        low = lax.rem(node, layer)
+        self.at = {"l": low, "c": lax.rem(low, 2), "y": low // 2, "z": node // layer, "x": grp}
 
     def member(self, axis, index):
-        at = dict(self.at)
-        at[axis] = index
-        return {"nodes": at["z"] * 4 + at["y"] * 2 + at["c"], "grp": at["x"]}
+        layer = self.size["l"]
+        low, line, grp = self.at["l"], self.at["z"], self.at["x"]
+        if axis == "l":
+            low = index
+        elif axis == "c":
+            low = self.at["y"] * 2 + index
+        elif axis == "y":
+            low = index * 2 + self.at["c"]
+        elif axis == "z":
+            line = index
+        else:
+            grp = index
+        return {"nodes": line * layer + low, "grp": grp}
 
     def others(self, axis):
         size = self.size[axis]
         for far in range(1, size):
             index = lax.rem(self.at[axis] + far, size)
             yield far - 1, index, self.member(axis, index)
+
+
+def remote(src, dst, send, recv, device):
+    return pltpu.make_async_remote_copy(
+        src_ref=src, dst_ref=dst, send_sem=send, recv_sem=recv, device_id=device, device_id_type=MESH
+    )
 
 
 def barrier(place, axes):
@@ -100,6 +82,580 @@
             pl.semaphore_signal(sem, inc=1, device_id=device, device_id_type=MESH)
             count += 1
     pl.semaphore_wait(sem, count)
+
+
+def gelu(v):
+    t = jnp.tanh(0.7978845608028654 * (v + 0.044715 * (v * v * v)))
+    return v * (0.5 * (1.0 + t))
+
+
+def gelu_slope(v):
+    square = v * v
+    t = jnp.tanh(0.7978845608028654 * (v + 0.044715 * (v * square)))
+    bend = 0.7978845608028654 * (1.0 + 0.134145 * square)
+    return 0.5 * (1.0 + t) + 0.5 * v * (1.0 - t * t) * bend
+
+
+class Share:
+    def __init__(self, place, bufs, send, recv):
+        self.place, self.send, self.recv = place, send, recv
+        self.stages, base = [], 0
+        for axis, buf in zip(("l", "z", "x"), bufs):
+            self.stages.append((axis, buf, base))
+            base += place.size[axis] - 1
+
+    def start(self, stage, value):
+        axis, buf, base = self.stages[stage]
+        me = self.place.at[axis]
+        buf[me] = value
+        for far, _, device in self.place.others(axis):
+            remote(
+                buf.at[me], buf.at[me], self.send.at[base + far], self.recv.at[base + far], device
+            ).start()
+
+    def finish(self, stage):
+        axis, buf, base = self.stages[stage]
+        me = self.place.at[axis]
+        for far, _, device in self.place.others(axis):
+            remote(
+                buf.at[me], buf.at[me], self.send.at[base + far], self.recv.at[base + far], device
+            ).wait()
+        total = buf[0]
+        for i in range(1, self.place.size[axis]):
+            total += buf[i]
+        return total
+
+
+def share_sems(n_nodes, n_grp):
+    return (n_nodes // LINE - 1) + (LINE - 1) + max(1, n_grp - 1)
+
+
+def forward_kernel(
+    n_nodes,
+    n_grp,
+    feats_h,
+    mask_ref,
+    keys_ref,
+    targets_ref,
+    board_h,
+    neigh_h,
+    nbias_ref,
+    comb_h,
+    cbias_ref,
+    cot_h,
+    embed_h,
+    hid_h,
+    pre_h,
+    featb_h,
+    board_b_h,
+    neigh_b_h,
+    comb1_b_h,
+    st_h,
+    dnum_h,
+    dz_h,
+    agg_h,
+    stats_ref,
+    stage,
+    featb,
+    hid,
+    pre,
+    board_b,
+    neigh_b,
+    comb_b,
+    keys,
+    msg,
+    acc,
+    spread,
+    spread_t,
+    out_slots,
+    in_slots,
+    out_tot,
+    in_tot,
+    picker,
+    num,
+    zval,
+    zpre,
+    cot,
+    agg,
+    dz,
+    dnum,
+    count_l,
+    count_z,
+    count_x,
+    load_sem,
+    store_sem,
+    key_send,
+    key_recv,
+    up_send,
+    down_send,
+    msg_recv,
+    slot_send,
+    slot_recv,
+    tot_send,
+    tot_recv,
+    count_send,
+    count_recv,
+):
+    place = Place(n_nodes, n_grp)
+    z, low = place.at["z"], place.at["l"]
+    layer = place.size["l"]
+    rows, width = featb.shape
+    edges = keys.shape[2]
+    layer_slots = spread.shape[1]
+    cap = layer_slots // layer
+    part = width // CHUNKS
+    turn = math.gcd(edges, 1024)
+    steps = edges // turn
+
+    sources = [feats_h.at[:]]
+    for whole in (board_h, neigh_h, comb_h):
+        for first in range(0, whole.shape[0], rows):
+            sources.append(whole.at[pl.ds(first, rows)])
+    n_stage = stage.shape[0]
+
+    def load(i):
+        return pltpu.make_async_copy(sources[i], stage.at[i % n_stage], load_sem.at[i % n_stage])
+
+    for i in range(n_stage):
+        load(i).start()
+    load_cot = pltpu.make_async_copy(cot_h, cot, load_sem.at[n_stage])
+    stores = []
+
+    def store(src, dst):
+        copy = pltpu.make_async_copy(src, dst, store_sem.at[len(stores)])
+        copy.start()
+        stores.append(copy)
+
+    barrier(place, ("l", "z", "x"))
+    keys[z] = keys_ref[...]
+
+    def key_copy(far, device):
+        return remote(keys.at[z], keys.at[z], key_send.at[far], key_recv.at[far], device)
+
+    for far, _, device in place.others("z"):
+        key_copy(far, device).start()
+    share = Share(place, (count_l, count_z, count_x), count_send, count_recv)
+    mask = mask_ref[...]
+    share.start(0, jnp.full((8, 128), jnp.sum(mask)))
+
+    def cast(i, target, first):
+        load(i).wait()
+        slot = stage.at[i % n_stage]
+
+        @pl.loop(0, rows // 32)
+        def _(r):
+            at = pl.ds(pl.multiple_of(r * 32, 32), 32)
+            to = pl.ds(pl.multiple_of(first + r * 32, 32), 32)
+            target[to, :] = slot[at, :].astype(BF16)
+
+    cast(0, featb, 0)
+    cast(1, board_b, 0)
+    cast(2, board_b, rows)
+
+    @pl.loop(0, CHUNKS)
+    def _(k):
+        at = pl.ds(pl.multiple_of(k * part, part), part)
+        proj = jnp.dot(featb[...], board_b[:, at], preferred_element_type=F32)
+        hid[:, at] = jnp.where(mask > 0.5, proj, stage[0, :, at]).astype(BF16)
+
+    cast(3, neigh_b, 0)
+    cast(4, neigh_b, rows)
+    for i in range(n_stage, len(sources)):
+        load(i).start()
+    load_cot.start()
+
+    def up_copy(src, k):
+        piece = msg.at[src, k]
+        index = src * CHUNKS + k
+        return remote(
+            piece, piece, up_send.at[index], msg_recv.at[index], place.member("z", z + 1)
+        )
+
+    def down_copy(src, k):
+        piece = msg.at[src, k]
+        index = src * CHUNKS + k
+        return remote(
+            piece, piece, down_send.at[index], msg_recv.at[index], place.member("z", z - 1)
+        )
+
+    @pl.loop(0, CHUNKS)
+    def _(k):
+        at = pl.ds(pl.multiple_of(k * part, part), part)
+        value = jnp.dot(hid[...], neigh_b[:, at], preferred_element_type=F32) + nbias_ref[:, at]
+        pre[:, at] = value
+        msg[z, k] = gelu(value).astype(BF16)
+
+        @pl.when(z < LINE - 1)
+        def _():
+            up_copy(z, k).start()
+
+        @pl.when(z > 0)
+        def _():
+            down_copy(z, k).start()
+
+    def forward(s):
+        k = lax.rem(s, CHUNKS)
+        below = z - 1 - s // CHUNKS
+        above = z + 1 + s // CHUNKS
+
+        @pl.when(below >= 0)
+        def _():
+            up_copy(below, k).wait_recv()
+
+            @pl.when(z < LINE - 1)
+            def _():
+                up_copy(below, k).start()
+
+        @pl.when(above < LINE)
+        def _():
+            down_copy(above, k).wait_recv()
+
+            @pl.when(z > 0)
+            def _():
+                down_copy(above, k).start()
+
+    def tot_copy(src, far, index, device):
+        at = (layer - 1) * src + far
+        return remote(
+            out_tot.at[src, pl.ds(pl.multiple_of(index * cap, cap), cap)],
+            in_tot.at[src, pl.ds(pl.multiple_of(low * cap, cap), cap)],
+            tot_send.at[at],
+            tot_recv.at[at],
+            device,
+        )
+
+    def finish_spread(src):
+        total = acc[...]
+        spread[src] = total.astype(BF16)
+        spread_t[src] = total.astype(BF16).T
+        sums = jnp.sum(total, axis=1, keepdims=True).astype(jnp.int32)
+        lane = lax.broadcasted_iota(jnp.int32, (layer_slots, 128), 1)
+        digit = jnp.where(
+            lane == 0, sums & 255, jnp.where(lane == 1, (sums >> 8) & 255, jnp.where(lane == 2, sums >> 16, 0))
+        )
+        out_tot[src] = digit.astype(F32).astype(BF16)
+        own = pl.ds(pl.multiple_of(low * cap, cap), cap)
+        in_tot[src, own] = out_tot[src, own]
+        for far, index, device in place.others("l"):
+            tot_copy(src, far, index, device).start()
+
+    early = {}
+    for s in range(CHUNKS * (LINE - 1)):
+        when = int((5.4 * (s + 1) + 3.0) / 0.36)
+        if when < LINE * steps:
+            early[s] = when
+
+    @pl.loop(0, LINE * steps)
+    def _(i):
+        which = i // steps
+        t = i - which * steps
+        src = lax.rem(z + which, LINE)
+
+        @pl.when(t == 0)
+        def _():
+            acc[...] = jnp.zeros_like(acc)
+
+        for far, index, device in place.others("z"):
+
+            @pl.when(jnp.logical_and(t == 0, which == far + 1))
+            def _(far=far):
+                remote(
+                    keys.at[src], keys.at[src], key_send.at[far], key_recv.at[LINE - 2 - far], device
+                ).wait_recv()
+
+        key = keys[src, :, pl.ds(pl.multiple_of(t * turn, turn), turn)]
+        weight = (key & 15).astype(F32).astype(F8)
+        child = (lax.shift_right_logical(key, 4) & (rows - 1)).astype(jnp.int16)
+        shift = 4 + int(math.log2(rows))
+        slot = (lax.shift_right_logical(key, shift) - z * layer_slots).astype(jnp.int16)
+        right = jnp.where(
+            lax.broadcasted_iota(jnp.int16, (rows, turn), 0) == child, weight, jnp.zeros((), F8)
+        )
+        block = 256
+        for first in range(0, layer_slots, block):
+            ids = lax.broadcasted_iota(jnp.int16, (block, turn), 0) + jnp.asarray(first, jnp.int16)
+            left = jnp.where(ids == slot, jnp.ones((), F8), jnp.zeros((), F8))
+            acc[pl.ds(first, block), :] += dot_nt(left, right)
+
+        @pl.when(t == steps - 1)
+        def _():
+            finish_spread(src)
+
+        for s, when in early.items():
+
+            @pl.when(i == when)
+            def _(s=s):
+                forward(s)
+
+        @pl.when(i == steps // 2)
+        def _():
+            share.start(1, share.finish(0))
+
+        @pl.when(i == steps)
+        def _():
+            share.start(2, share.finish(1))
+
+    boards = share.finish(2)[0:1, 0:1]
+    scale = 1.0 / (width * (1.0 + boards))
+
+    def slot_copy(src, k, far, index, device):
+        at = (src * CHUNKS + k) * (layer - 1) + far
+        return remote(
+            out_slots.at[src, k, pl.ds(pl.multiple_of(index * cap, cap), cap)],
+            in_slots.at[src, k, pl.ds(pl.multiple_of(low * cap, cap), cap)],
+            slot_send.at[at],
+            slot_recv.at[at],
+            device,
+        )
+
+    def piece(src, k):
+        out_slots[src, k] = jnp.dot(spread[src], msg[src, k], preferred_element_type=F32).astype(BF16)
+        for far, index, device in place.others("l"):
+            slot_copy(src, k, far, index, device).start()
+        own = pl.ds(pl.multiple_of(low * cap, cap), cap)
+        in_slots[src, k, own] = out_slots[src, k, own]
+
+    def pick(src, k):
+        for far, index, device in place.others("l"):
+            slot_copy(src, k, far, index, device).wait_recv()
+        num[k] += jnp.dot(picker[src], in_slots[src, k], preferred_element_type=F32)
+
+    @pl.loop(0, CHUNKS)
+    def _(k):
+        piece(z, k)
+
+    def both(j, act, k):
+        @pl.when(z - 1 - j >= 0)
+        def _():
+            act(z - 1 - j, k)
+
+        @pl.when(z + 1 + j < LINE)
+        def _():
+            act(z + 1 + j, k)
+
+    def arrive(j, k):
+        s = j * CHUNKS + k
+        for done in range(CHUNKS):
+            if j * CHUNKS + done not in early:
+
+                @pl.when(k == done)
+                def _(done=done):
+                    forward(j * CHUNKS + done)
+
+        both(j, piece, k)
+
+    @pl.loop(0, CHUNKS)
+    def _(k):
+        arrive(0, k)
+
+    num[...] = jnp.zeros_like(num)
+
+    @pl.loop(0, LINE)
+    def _(src):
+        at = pl.ds(pl.multiple_of(src * layer_slots, layer_slots), layer_slots)
+        ids = lax.broadcasted_iota(jnp.int32, (rows, layer_slots), 0)
+        picker[src] = jnp.where(ids == targets_ref[:, at], 1.0, 0.0).astype(BF16)
+
+    for i in range(5, 5 + 2 * width // rows):
+        cast(i, comb_b, (i - 5) * rows)
+
+    @pl.loop(0, CHUNKS)
+    def _(k):
+        at = pl.ds(pl.multiple_of(k * part, part), part)
+        zpre[:, at] = (
+            jnp.dot(hid[...], comb_b[0:width, at], preferred_element_type=F32) + cbias_ref[:, at]
+        )
+
+    store(hid, hid_h)
+    store(pre, pre_h)
+    store(featb, featb_h)
+    store(board_b, board_b_h)
+    store(neigh_b, neigh_b_h)
+    store(comb_b.at[pl.ds(0, width)], comb1_b_h)
+    store(spread_t, st_h)
+
+    @pl.loop(0, CHUNKS)
+    def _(k):
+        pick(z, k)
+
+    for j in range(1, LINE - 1):
+
+        @pl.loop(0, CHUNKS)
+        def _(k):
+            both(j - 1, pick, k)
+            arrive(j, k)
+
+    den_digits = jnp.zeros((rows, 128), F32)
+    for src in range(LINE):
+        for far, index, device in place.others("l"):
+            tot_copy(src, far, index, device).wait_recv()
+        den_digits += jnp.dot(picker[src], in_tot[src], preferred_element_type=F32)
+    lane = lax.broadcasted_iota(jnp.int32, (rows, 128), 1)
+    worth = jnp.where(lane == 0, 1.0, jnp.where(lane == 1, 256.0, jnp.where(lane == 2, 65536.0, 0.0)))
+    den = 1.0 + jnp.sum(den_digits * worth, axis=1, keepdims=True)
+    load_cot.wait()
+
+    @pl.loop(0, CHUNKS)
+    def _(k):
+        both(LINE - 2, pick, k)
+
+    @pl.loop(0, CHUNKS)
+    def _(k):
+        at = pl.ds(pl.multiple_of(k * part, part), part)
+        agg[:, at] = (num[k] / den).astype(BF16)
+
+    def dense(k, carry):
+        square, along = carry
+        at = pl.ds(pl.multiple_of(k * part, part), part)
+        value = zpre[:, at] + jnp.dot(
+            agg[...], comb_b[width : 2 * width, at], preferred_element_type=F32
+        )
+        zpre[:, at] = value
+        out = gelu(value)
+        zval[:, at] = out
+        square += jnp.sum(out * out, axis=1, keepdims=True)
+        along += jnp.sum(out * cot[:, at], axis=1, keepdims=True)
+        return square, along
+
+    zero = jnp.zeros((rows, 1), F32)
+    square, along = lax.fori_loop(0, CHUNKS, dense, (zero, zero))
+    inverse = lax.rsqrt(square + 1e-06)
+    along = along * inverse
+    push = jnp.where(mask > 0.5, 2.0 * scale, 0.0)
+    stats_ref[...] = jnp.concatenate(
+        [
+            jnp.full((8, 128), jnp.sum(jnp.where(mask > 0.5, square, 0.0))),
+            jnp.broadcast_to(scale, (8, 128)),
+        ],
+        axis=0,
+    )
+
+    @pl.loop(0, CHUNKS)
+    def _(k):
+        at = pl.ds(pl.multiple_of(k * part, part), part)
+        out = zval[:, at]
+        emb = out * inverse
+        grad = inverse * (cot[:, at] - emb * along) + push * out
+        dz[:, at] = (grad * gelu_slope(zpre[:, at])).astype(BF16)
+        zval[:, at] = emb
+
+    store(zval, embed_h)
+    store(dz, dz_h)
+    store(agg, agg_h)
+
+    @pl.loop(0, CHUNKS)
+    def _(k):
+        at = pl.ds(pl.multiple_of(k * part, part), part)
+        back = dot_nt(dz[...], comb_b[pl.ds(pl.multiple_of(width + k * part, part), part), :])
+        dnum[:, at] = (back / den).astype(BF16)
+
+    store(dnum, dnum_h)
+
+    for far, _, device in place.others("z"):
+        key_copy(far, device).wait_send()
+
+    @pl.loop(0, LINE * CHUNKS)
+    def _(i):
+        src = i // CHUNKS
+        k = lax.rem(i, CHUNKS)
+
+        @pl.when(jnp.logical_and(src <= z, z < LINE - 1))
+        def _():
+            up_copy(src, k).wait_send()
+
+        @pl.when(jnp.logical_and(src >= z, z > 0))
+        def _():
+            down_copy(src, k).wait_send()
+
+        for far, index, device in place.others("l"):
+            slot_copy(src, k, far, index, device).wait_send()
+
+    for src in range(LINE):
+        for far, index, device in place.others("l"):
+            tot_copy(src, far, index, device).wait_send()
+    for copy in stores:
+        copy.wait()
+
+
+def forward_pass(n_nodes, n_grp, feats, mask, keys, targets, board, neigh, nbias, comb, cbias, cot):
+    rows, width = feats.shape
+    edges = keys.shape[1]
+    layer = n_nodes // LINE
+    layer_slots = targets.shape[1] // LINE
+    part = width // CHUNKS
+    dma = pltpu.SemaphoreType.DMA
+    n_stage = 5
+    big = pl.BlockSpec(memory_space=pl.ANY)
+    small = pl.BlockSpec(memory_space=pltpu.VMEM)
+
+    def hbm(shape, dtype):
+        return jax.ShapeDtypeStruct(shape, dtype)
+
+    return pl.pallas_call(
+        functools.partial(forward_kernel, n_nodes, n_grp),
+        out_shape=[
+            hbm((rows, width), F32),
+            hbm((rows, width), BF16),
+            hbm((rows, width), F32),
+            hbm((rows, width), BF16),
+            hbm((width, width), BF16),
+            hbm((width, width), BF16),
+            hbm((width, width), BF16),
+            hbm((LINE, rows, layer_slots), BF16),
+            hbm((rows, width), BF16),
+            hbm((rows, width), BF16),
+            hbm((rows, width), BF16),
+            hbm((16, 128), F32),
+        ],
+        in_specs=[big, small, small, small, big, big, small, big, small, big],
+        out_specs=[big] * 11 + [small],
+        scratch_shapes=[
+            pltpu.VMEM((n_stage, rows, width), F32),
+            pltpu.VMEM((rows, width), BF16),
+            pltpu.VMEM((rows, width), BF16),
+            pltpu.VMEM((rows, width), F32),
+            pltpu.VMEM((width, width), BF16),
+            pltpu.VMEM((width, width), BF16),
+            pltpu.VMEM((2 * width, width), BF16),
+            pltpu.VMEM((LINE, 1, edges), jnp.int32),
+            pltpu.VMEM((LINE, CHUNKS, rows, part), BF16),
+            pltpu.VMEM((layer_slots, rows), F32),
+            pltpu.VMEM((LINE, layer_slots, rows), BF16),
+            pltpu.VMEM((LINE, rows, layer_slots), BF16),
+            pltpu.VMEM((LINE, CHUNKS, layer_slots, part), BF16),
+            pltpu.VMEM((LINE, CHUNKS, layer_slots, part), BF16),
+            pltpu.VMEM((LINE, layer_slots, 128), BF16),
+            pltpu.VMEM((LINE, layer_slots, 128), BF16),
+            pltpu.VMEM((LINE, rows, layer_slots), BF16),
+            pltpu.VMEM((CHUNKS, rows, part), F32),
+            pltpu.VMEM((rows, width), F32),
+            pltpu.VMEM((rows, width), F32),
+            pltpu.VMEM((rows, width), F32),
+            pltpu.VMEM((rows, width), BF16),
+            pltpu.VMEM((rows, width), BF16),
+            pltpu.VMEM((rows, width), BF16),
+            pltpu.VMEM((layer, 8, 128), F32),
+            pltpu.VMEM((LINE, 8, 128), F32),
+            pltpu.VMEM((n_grp, 8, 128), F32),
+            dma((n_stage + 1,)),
+            dma((11,)),
+            dma((LINE - 1,)),
+            dma((LINE - 1,)),
+            dma((LINE * CHUNKS,)),
+            dma((LINE * CHUNKS,)),
+            dma((LINE * CHUNKS,)),
+            dma((LINE * CHUNKS * (layer - 1),)),
+            dma((LINE * CHUNKS * (layer - 1),)),
+            dma((LINE * (layer - 1),)),
+            dma((LINE * (layer - 1),)),
+            dma((share_sems(n_nodes, n_grp),)),
+            dma((share_sems(n_nodes, n_grp),)),
+        ],
+        compiler_params=pltpu.CompilerParams(
+            vmem_limit_bytes=60 * MIB, collective_id=2, has_side_effects=True
+        ),
+        name="forward_pass",
+    )(feats, mask, keys, targets, board, neigh, nbias, comb, cbias, cot)
 
 
 def add_into(target, first, count, columns, parts, step=16):
@@ -198,7 +754,7 @@
 
 
 def job_sems(n_nodes, n_grp):
-    return 2 * (1 + (2 - 1) + (n_nodes // 4 - 1) + (n_grp - 1))
+    return 2 * (1 + (n_nodes // LINE // 2 - 1) + (LINE - 1) + (n_grp - 1))
 
 
 def run_jobs(jobs, at_once):
@@ -299,59 +855,49 @@
     out_cot,
 ):
     feats = features[0]
-    board = (type_mask[0] == 1)[:, None]
     rows, width = feats.shape
     peers = recv_rows.shape[2]
     cap = recv_rows.shape[3]
+    layer = n_nodes // LINE
     slots = peers * cap
-    board_count = lax.psum(jnp.sum(type_mask[0]).astype(F32), ("nodes", "grp"))
-    scale = 1.0 / (width * (1.0 + board_count))
-    spread = build_spread(edge_slot[0], edge_child[0], edge_weight[0], slots, rows)
-    totals = jnp.sum(spread, axis=1).astype(jnp.int32).reshape(peers, cap)
-    arrived_tot = lax.all_to_all(totals, "nodes", split_axis=0, concat_axis=0, tiled=True)
-    pbl = board_proj.astype(BF16)
-    qwl = neigh_proj.astype(BF16)
-    cwl = combine_proj.astype(BF16)
-    featb = feats.astype(BF16)
-    proj = jnp.dot(featb, pbl, preferred_element_type=F32)
-    hidden = jnp.where(board, proj, feats).astype(BF16)
-    pre = jnp.dot(hidden, qwl, preferred_element_type=F32) + neigh_bias
-    message, gelu_msg = jax.vjp(gelu_tanh, pre)
-    spread_b = spread.astype(BF16)
-    slot_sums = jnp.dot(spread_b, message.astype(BF16), preferred_element_type=F32)
-    slot_sums = slot_sums.astype(BF16).reshape(peers, cap, width)
-    arrived = lax.all_to_all(slot_sums, "nodes", split_axis=0, concat_axis=0, tiled=True)
-    targets = recv_rows[0, 0].reshape(-1)
-    picker_bool = targets[None, :] == jnp.arange(rows, dtype=jnp.int32)[:, None]
-    picker = picker_bool.astype(BF16)
-    num = jnp.dot(picker, arrived.reshape(slots, width), preferred_element_type=F32)
-    den = 1.0 + jnp.dot(
-        picker_bool.astype(F32), arrived_tot.reshape(-1).astype(F32), precision=HIGH
-    )
-    aggb = (num / den[:, None]).astype(BF16)
-    zpre = jnp.dot(hidden, cwl[:width], preferred_element_type=F32)
-    zpre = zpre + jnp.dot(aggb, cwl[width:], preferred_element_type=F32) + combine_bias
-    zval, gelu_z = jax.vjp(gelu_tanh, zpre)
-    sumsq = jnp.sum(zval * zval, axis=1)
-    inverse = lax.rsqrt(sumsq + 1e-06)
-    embed = zval * inverse[:, None]
-    board_sq = jnp.sum(jnp.where(board[:, 0], sumsq, 0.0))
-    cot = out_cot[0]
-    dz = inverse[:, None] * (cot - embed * jnp.sum(cot * embed, axis=1, keepdims=True))
-    dz = dz + jnp.where(board, 2.0 * scale * zval, 0.0)
-    dzb = gelu_z(dz)[0].astype(BF16)
+    mask = type_mask[0].astype(F32).reshape(rows, 1)
+    board = mask > 0.5
+    keys = ((edge_slot[0] * rows + edge_child[0]) * 16 + edge_weight[0]).reshape(1, -1)
+    targets = recv_rows[0, 0].reshape(1, slots)
+    embed, hidden, pre, featb, pbl, qwl, cwl1, spread_t, dnum, dzb, aggb, stats = forward_pass(
+        n_nodes,
+        n_grp,
+        feats,
+        mask,
+        keys,
+        targets,
+        board_proj,
+        neigh_proj,
+        neigh_bias.reshape(1, width),
+        combine_proj,
+        combine_bias.reshape(1, width),
+        out_cot[0],
+    )
+    board_sq = stats[0, 0]
+    scale = stats[8, 0]
     joined = jnp.concatenate([hidden, aggb], axis=1)
     grad_comb = dot_tn(joined, dzb).astype(BF16)
     grad_cbias = jnp.sum(dzb.astype(F32), axis=0)
-    dcat = dot_nt(dzb, cwl)
-    dnum = (dcat[:, width:] / den[:, None]).astype(BF16)
-    back_slots = dot_tn(picker, dnum).astype(BF16).reshape(peers, cap, width)
-    returned = lax.all_to_all(back_slots, "nodes", split_axis=0, concat_axis=0, tiled=True)
-    dmsg = dot_tn(spread_b, returned.reshape(slots, width))
-    dpre = gelu_msg(dmsg)[0].astype(BF16)
+    picker = (targets[0][None, :] == jnp.arange(rows, dtype=jnp.int32)[:, None]).astype(BF16)
+    back_slots = dot_tn(picker, dnum).astype(BF16).reshape(LINE, layer, cap, width)
+    layers = [[i * layer + j for j in range(layer)] for i in range(LINE)]
+    lines = [[i * layer + j for i in range(LINE)] for j in range(layer)]
+    returned = lax.all_to_all(
+        back_slots, "nodes", split_axis=1, concat_axis=1, tiled=True, axis_index_groups=layers
+    ).reshape(LINE, layer * cap, width)
+    partial = jnp.einsum("zcs,zsd->zcd", spread_t, returned, preferred_element_type=F32)
+    dmsg = lax.psum_scatter(
+        partial, "nodes", scatter_dimension=0, axis_index_groups=lines, tiled=False
+    )
+    dpre = (dmsg * gelu_slope(pre)).astype(BF16)
     grad_qbias = jnp.sum(dpre.astype(F32), axis=0)
     grad_neigh = dot_tn(hidden, dpre).astype(BF16)
-    dhid = (dcat[:, :width] + dot_nt(dpre, qwl)).astype(BF16)
+    dhid = (dot_nt(dzb, cwl1) + dot_nt(dpre, qwl)).astype(BF16)
     dproj = jnp.where(board, dhid, jnp.zeros_like(dhid))
     grad_board = dot_tn(featb, dproj).astype(BF16)
     grad_feats = jnp.where(board, dot_nt(dproj, pbl), dhid.astype(F32))

time: 465 us -> 527 us (1.13)
  Pallas kernels: 132 us -> 229 us
  waiting for transfers between devices: 71.8 us -> 135 us
  blocking collectives: 152 us -> 92.8 us
  matrix products: 46.2 us -> 24.3 us
  starting transfers between devices: 19.1 us -> 0.04 us
  between operations: 4.1 us -> 16.6 us
  other arithmetic: 30.1 us -> 20.8 us
    reduce_scatter x0 -> x1, waiting for transfers between devices: none -> 135 us  [on_device(): lax.psum_scatter(partial, 'nodes', scatter_dimension=0, axis_index_groups...]
    psum x1 -> x0, blocking collectives: 113 us -> none  [on_device(): board_count = lax.psum(jnp.sum(type_mask[0]).astype(F32), ('nodes', 'grp'))]
    pallas_call x1, Pallas kernels: 31.5 us -> 143 us  [forward_pass(): pl.pallas_call(functools.partial(forward_kernel, n_nodes, n_grp), out_sha...]
    all_to_all x3 -> x0, waiting for transfers between devices: 71.8 us -> none  [the longest x1 71.8 us: on_device(): lax.all_to_all(back_slots, 'nodes', split_axis=0, concat_axis=0, tiled=True)]
    all_to_all x0 -> x1, blocking collectives: none -> 51.5 us  [on_device(): lax.all_to_all(back_slots, 'nodes', split_axis=1, concat_axis=1, tiled=Tr...]
    all_to_all x3 -> x0, starting transfers between devices: 19.1 us -> none  [the longest x1 7.39 us: on_device(): lax.all_to_all(totals, 'nodes', split_axis=0, concat_axis=0, tiled=True)]
    pallas_call x1, Pallas kernels: 100 us -> 85.7 us  [all_reduce(): pl.pallas_call(functools.partial(reduce_kernel, n_nodes, n_grp, count), o...]
    dot_general x7 -> x1, matrix products: 19.2 us -> 5.75 us  [on_device(): jnp.einsum('zcs,zsd->zcd', spread_t, returned, preferred_element_type=F32)]
  transfers between devices with their start and end apart: 3 -> 1, of which waited for: 1 -> 1; matrix products, arithmetic and copies ran while one was open for 5% -> 2% of each run, Pallas kernels for 0% -> 0%
where the time goes in v2:
time: 527 us
  Pallas kernels  229 us (43%)
  waiting for transfers between devices  135 us (26%)
  blocking collectives  92.8 us (18%)
  matrix products  24.3 us (5%)
  other arithmetic  20.8 us (4%)
  between operations  16.6 us (3%)
  local copies, waits for them, and re-layouts  8.7 us (2%)
    pallas_call x1, Pallas kernels, forward_pass(): pl.pallas_call(functools.partial(forward_kernel, n_nodes, n_grp), out_sha...  143 us
    reduce_scatter x1, waiting for transfers between devices, on_device(): lax.psum_scatter(partial, 'nodes', scatter_dimension=0, axis_index_groups...  135 us
    pallas_call x1, Pallas kernels, all_reduce(): pl.pallas_call(functools.partial(reduce_kernel, n_nodes, n_grp, count), o...  85.7 us
    all_to_all x1, blocking collectives, on_device(): lax.all_to_all(back_slots, 'nodes', split_axis=1, concat_axis=1, tiled=Tr...  51.5 us
    psum x1, blocking collectives, on_device(): lax.psum(jnp.concatenate([grad_qbias, grad_cbias, jnp.full((width,), boar...  41.4 us
    dot_general x4, matrix products, dot_tn(): lax.dot_general(left, right, (((0,), (0,)), ((), ())), preferred_element_...  12 us
  transfers between devices with their start and end apart: 1, of which 1 were waited for; matrix products, arithmetic and copies ran while one was open for 2% of the time, Pallas kernels for 0%

profile of v2, /device:TPU:0, one launch (start us, length us, event | category | flops | bytes accessed | tf_op | source)
XLA Modules:
  0.0 526.8 jit_solution(12453834655509545256)
XLA Ops:
  7.2 0.7 convert_bitcast_fusion
  7.9 0.9 copy.21.mask_ref
  8.8 1.8 multiply_add_fusion.keys_ref
  10.6 143.0 %forward_pass.1 = (f32[512,1024]{1,0:T(8,128)}, bf16[512,1024]{1,0:T(8,128)(2,1)}, f32[512,1024]{1,0:T(8,128)}, bf16[512,1024]{1,0:T(8,128)(2,1)}, bf16[1024,102...) custom-call(f32[512,1024]{1,0:T(8,128)} %bitcast.33, ...), custom_call_target="tpu_custom_call" | custom-call | tf_op jit(solution)/shard_map/forward_pass/pallas_call | solution.py:594
  153.6 3.6 fusion.1
  157.8 51.5 %all_to_all.5 = bf16[4,4,128,1024]{3,2,0,1:T(8,128)(2,1)S(1)} all-to-all(bf16[4,4,128,1024]{3,2,0,1:T(8,128)(2,1)S(1)} %copy.22), channel_id=1, replica_groups={{0,2,4,6},{8,10,12,14},{16,18,20,22},{24,26,28,30},{1,3,5,7},{9,11,13,1..., dimensions={1} | all-to-all | bytes 8388608 | tf_op jit(solution)/shard_map/all_to_all | solution.py:890
  209.9 1.0 copy-done.2
  210.9 5.7 %fusion.24 = f32[4,512,1024]{2,1,0:T(8,128)} fusion(bf16[4,512,512]{2,1,0:T(8,128)(2,1)S(1)} %copy-done.2, bf16[4,512,1024]{2,1,0:T(8,128)(2,1)S(1)} %bitcast.31), kind=kOutput, calls=%fused_computation.42 | convolution fusion | flops 2147483648 | bytes 14680064 | tf_op jit(solution)/shard_map/zcs,zsd->zcd/dot_general | solution.py:893
  216.7 1.4 fusion.23
  218.6 2.6 fusion.25
  221.2 4.4 convolution_convert_fusion
  225.6 134.7 %reduce-scatter.2.cloned.1.call-done = f32[1,512,1024]{2,1,0:T(8,128)} async-done(((f32[4,512,1024]{2,1,0:T(8,128)}), f32[1,512,1024]{2,1,0:T(8,128)}) %reduce-scatter.2.cloned.1.call-update) | async-done | bytes 2097168 | tf_op jit(solution)/shard_map/reduce_scatter | solution.py:894
  360.3 2.9 convert_reduce_fusion.1
  363.9 41.4 %psum.7 = f32[3072]{0:T(1024)S(1)} all-reduce(f32[3072]{0:T(1024)S(1)} %pad_maximum_fusion.1), channel_id=1, replica_groups=mesh['nodes'=16,'grp'=2] {'nodes','grp'}, use_global_device_ids=true, to_apply=%region_3.4 | all-reduce | flops 3072 | bytes 24576 | tf_op jit(solution)/shard_map/psum | solution.py:904
  406.4 2.7 convolution_convert_fusion.2
  409.1 1.3 add_convert_fusion
  410.4 1.3 convolution_convert_fusion.1
  411.8 0.8 copy-done.1
  412.6 3.9 pad_maximum_fusion.grad_hbm
  416.5 85.7 %sum_gradients.1 = bf16[4096,1024]{1,0:T(8,128)(2,1)} custom-call(bf16[4096,1024]{1,0:T(8,128)(2,1)} %pad_maximum_fusion.grad_hbm), custom_call_target="tpu_custom_call" | custom-call | tf_op jit(solution)/shard_map/sum_gradients/pallas_call | solution.py:819
  502.2 6.8 %slice_convert_fusion.1 = (f32[1024,1024]{1,0:T(8,128)}, f32[1024,1024]{1,0:T(8,128)}) fusion(bf16[4096,1024]{1,0:T(8,128)(2,1)} %sum_gradients.1), kind=kLoop, calls=%fused_computation.21 | loop fusion | flops 2097152 | bytes 12582912 | tf_op jit(solution)/shard_map/convert_element_type | solution.py:916
  509.1 4.4 slice_convert_fusion
  513.5 2.6 select_bitcast_fusion
  517.5 1.3 copy.25
  (38 shorter events, 3.6 us)
Async XLA Ops:
  7.2 353.2 %reduce-scatter.2.cloned.1.call-start = ((), (), s32[]{:S(2)}) async-start(), calls=%async_computation.2 | async-start | bytes 10485760 | tf_op jit(solution)/shard_map/reduce_scatter | solution.py:894
  10.6 143.0 %copy-start.6 = (s32[1,1,16,128]{3,2,1,0:T(8,128)S(1)}, s32[1,1,16,128]{3,2,1,0:T(8,128)}, u32[]{:S(2)}) copy-start(s32[1,1,16,128]{3,2,1,0:T(8,128)} %param.17) | copy-start | bytes 24580
  209.3 1.6 copy-start.2
  216.7 1.4 copy-start.7
  216.7 1.4 copy-start.5
  216.7 1.9 copy-start.10
  218.6 2.6 copy-start.12
  218.6 2.6 copy-start.13
  221.2 139.1 %copy-start.4 = (f32[512,1024]{1,0:T(8,128)S(1)}, f32[512,1024]{1,0:T(8,128)}, u32[]{:S(2)}) copy-start(f32[512,1024]{1,0:T(8,128)} %get-tuple-element.23) | copy-start | bytes 6291460
  406.4 2.7 copy-start.9
  406.4 2.7 copy-start.14
  409.1 1.3 copy-start.11
  410.4 2.2 copy-start.1
  502.2 6.8 %copy-start = (bf16[4096,1024]{1,0:T(8,128)(2,1)S(1)}, bf16[4096,1024]{1,0:T(8,128)(2,1)}, u32[]{:S(2)}) copy-start(bf16[4096,1024]{1,0:T(8,128)(2,1)} %sum_gradients.1) | copy-start | bytes 25165828
  509.1 4.4 copy-start.8
  513.5 3.9 copy-start.3
Sparse Core Ops, SparseCore 0:
  216.8 143.4 reduce-scatter.1

commit v3 on v2

--- a/solution.py
+++ b/solution.py
@@ -34,6 +34,7 @@
 
 LINE = 4
 CHUNKS = 4
+ORDER = ((0, 1, 2, 3), (1, 2, 0, 3))
 
 
 class Place:
@@ -204,7 +205,7 @@
     layer_slots = spread.shape[1]
     cap = layer_slots // layer
     part = width // CHUNKS
-    turn = math.gcd(edges, 1024)
+    turn = math.gcd(edges, 2560)
     steps = edges // turn
 
     sources = [feats_h.at[:]]
@@ -339,64 +340,45 @@
         for far, index, device in place.others("l"):
             tot_copy(src, far, index, device).start()
 
-    early = {}
-    for s in range(CHUNKS * (LINE - 1)):
-        when = int((5.4 * (s + 1) + 3.0) / 0.36)
-        if when < LINE * steps:
-            early[s] = when
-
-    @pl.loop(0, LINE * steps)
-    def _(i):
-        which = i // steps
-        t = i - which * steps
-        src = lax.rem(z + which, LINE)
-
-        @pl.when(t == 0)
-        def _():
-            acc[...] = jnp.zeros_like(acc)
-
-        for far, index, device in place.others("z"):
-
-            @pl.when(jnp.logical_and(t == 0, which == far + 1))
-            def _(far=far):
-                remote(
-                    keys.at[src], keys.at[src], key_send.at[far], key_recv.at[LINE - 2 - far], device
-                ).wait_recv()
-
-        key = keys[src, :, pl.ds(pl.multiple_of(t * turn, turn), turn)]
-        weight = (key & 15).astype(F32).astype(F8)
-        child = (lax.shift_right_logical(key, 4) & (rows - 1)).astype(jnp.int16)
-        shift = 4 + int(math.log2(rows))
-        slot = (lax.shift_right_logical(key, shift) - z * layer_slots).astype(jnp.int16)
-        right = jnp.where(
-            lax.broadcasted_iota(jnp.int16, (rows, turn), 0) == child, weight, jnp.zeros((), F8)
-        )
-        block = 256
-        for first in range(0, layer_slots, block):
-            ids = lax.broadcasted_iota(jnp.int16, (block, turn), 0) + jnp.asarray(first, jnp.int16)
-            left = jnp.where(ids == slot, jnp.ones((), F8), jnp.zeros((), F8))
-            acc[pl.ds(first, block), :] += dot_nt(left, right)
-
-        @pl.when(t == steps - 1)
-        def _():
-            finish_spread(src)
-
-        for s, when in early.items():
-
-            @pl.when(i == when)
-            def _(s=s):
-                forward(s)
-
-        @pl.when(i == steps // 2)
-        def _():
-            share.start(1, share.finish(0))
-
-        @pl.when(i == steps)
-        def _():
-            share.start(2, share.finish(1))
-
-    boards = share.finish(2)[0:1, 0:1]
-    scale = 1.0 / (width * (1.0 + boards))
+    def source(which):
+        flip = z // 2
+        inner = z * (1 - 2 * flip) + (LINE - 1) * flip
+        index = ORDER[0][which] * (1 - inner) + ORDER[1][which] * inner
+        return index * (1 - 2 * flip) + (LINE - 1) * flip
+
+    def build(which, ticks):
+        src = source(which)
+        acc[...] = jnp.zeros_like(acc)
+        if which > 0:
+            far = lax.rem(z - src - 1 + LINE, LINE)
+            remote(
+                keys.at[src], keys.at[src], key_send.at[0], key_recv.at[far], place.member("z", src)
+            ).wait_recv()
+
+        @pl.loop(0, steps)
+        def _(t):
+            key = keys[src, :, pl.ds(pl.multiple_of(t * turn, turn), turn)]
+            weight = (key & 15).astype(F32).astype(F8)
+            child = (lax.shift_right_logical(key, 4) & (rows - 1)).astype(jnp.int16)
+            shift = 4 + int(math.log2(rows))
+            slot = (lax.shift_right_logical(key, shift) - z * layer_slots).astype(jnp.int16)
+            right = jnp.where(
+                lax.broadcasted_iota(jnp.int16, (rows, turn), 0) == child, weight, jnp.zeros((), F8)
+            )
+            block = 256
+            for first in range(0, layer_slots, block):
+                ids = lax.broadcasted_iota(jnp.int16, (block, turn), 0) + jnp.asarray(
+                    first, jnp.int16
+                )
+                left = jnp.where(ids == slot, jnp.ones((), F8), jnp.zeros((), F8))
+                acc[pl.ds(first, block), :] += dot_nt(left, right)
+            for share_of_loop, act in ticks:
+
+                @pl.when(t == min(steps - 1, int(share_of_loop * steps)))
+                def _(act=act):
+                    act()
+
+        finish_spread(src)
 
     def slot_copy(src, k, far, index, device):
         at = (src * CHUNKS + k) * (layer - 1) + far
@@ -420,41 +402,44 @@
             slot_copy(src, k, far, index, device).wait_recv()
         num[k] += jnp.dot(picker[src], in_slots[src, k], preferred_element_type=F32)
 
-    @pl.loop(0, CHUNKS)
-    def _(k):
-        piece(z, k)
-
-    def both(j, act, k):
-        @pl.when(z - 1 - j >= 0)
-        def _():
-            act(z - 1 - j, k)
-
-        @pl.when(z + 1 + j < LINE)
-        def _():
-            act(z + 1 + j, k)
-
-    def arrive(j, k):
-        s = j * CHUNKS + k
-        for done in range(CHUNKS):
-            if j * CHUNKS + done not in early:
-
-                @pl.when(k == done)
-                def _(done=done):
-                    forward(j * CHUNKS + done)
-
-        both(j, piece, k)
-
-    @pl.loop(0, CHUNKS)
-    def _(k):
-        arrive(0, k)
-
-    num[...] = jnp.zeros_like(num)
+    def each(act, which, first, last):
+        src = source(which)
+
+        @pl.loop(first, last)
+        def _(k):
+            act(src, k)
+
+    build(0, [(0.7, lambda: forward(0))])
+    each(piece, 0, 0, CHUNKS)
+
+    def second():
+        forward(1)
+        share.start(1, share.finish(0))
+
+    build(1, [(0.3, second), (0.9, lambda: forward(2))])
+    each(piece, 1, 0, CHUNKS - 1)
+
+    def third():
+        forward(3)
+        share.start(2, share.finish(1))
+
+    build(2, [(0.3, third), (0.9, lambda: forward(4))])
+    each(piece, 1, CHUNKS - 1, CHUNKS)
+    each(piece, 2, 0, 1)
+    build(3, [(0.5, lambda: forward(5)), (0.9, lambda: forward(6))])
+    each(piece, 2, 1, 3)
 
     @pl.loop(0, LINE)
     def _(src):
         at = pl.ds(pl.multiple_of(src * layer_slots, layer_slots), layer_slots)
         ids = lax.broadcasted_iota(jnp.int32, (rows, layer_slots), 0)
         picker[src] = jnp.where(ids == targets_ref[:, at], 1.0, 0.0).astype(BF16)
+
+    num[...] = jnp.zeros_like(num)
+    boards = share.finish(2)[0:1, 0:1]
+    scale = 1.0 / (width * (1.0 + boards))
+    forward(7)
+    each(piece, 2, 3, 4)
 
     for i in range(5, 5 + 2 * width // rows):
         cast(i, comb_b, (i - 5) * rows)
@@ -473,18 +458,16 @@
     store(neigh_b, neigh_b_h)
     store(comb_b.at[pl.ds(0, width)], comb1_b_h)
     store(spread_t, st_h)
-
-    @pl.loop(0, CHUNKS)
-    def _(k):
-        pick(z, k)
-
-    for j in range(1, LINE - 1):
-
-        @pl.loop(0, CHUNKS)
-        def _(k):
-            both(j - 1, pick, k)
-            arrive(j, k)
-
+    each(pick, 0, 0, CHUNKS)
+    forward(8)
+    each(piece, 3, 0, 1)
+    each(pick, 1, 0, CHUNKS)
+    forward(9)
+    each(piece, 3, 1, 2)
+    each(pick, 2, 0, CHUNKS)
+    forward(10)
+    each(piece, 3, 2, 3)
+    each(pick, 3, 0, 1)
     den_digits = jnp.zeros((rows, 128), F32)
     for src in range(LINE):
         for far, index, device in place.others("l"):
@@ -495,9 +478,9 @@
     den = 1.0 + jnp.sum(den_digits * worth, axis=1, keepdims=True)
     load_cot.wait()
 
-    @pl.loop(0, CHUNKS)
-    def _(k):
-        both(LINE - 2, pick, k)
+    forward(11)
+    each(piece, 3, 3, 4)
+    each(pick, 3, 1, 4)
 
     @pl.loop(0, CHUNKS)
     def _(k):
@@ -757,85 +740,448 @@
     return 2 * (1 + (n_nodes // LINE // 2 - 1) + (LINE - 1) + (n_grp - 1))
 
 
-def run_jobs(jobs, at_once):
-    waiting, running = list(jobs), []
-    while waiting or running:
+class Line:
+    def __init__(self):
+        self.running = []
+
+    def add(self, job):
+        next(job)
+        self.running.append(job)
+
+    def tick(self):
         left = []
-        for job in running:
+        for job in self.running:
             try:
                 next(job)
                 left.append(job)
             except StopIteration:
                 pass
-        for job in waiting[:at_once]:
-            next(job)
-            left.append(job)
-        waiting = waiting[at_once:]
-        running = left
-
-
-def reduce_kernel(n_nodes, n_grp, count, grad_hbm, out_hbm, grad, out, arrive, land, send, recv, sem_in, sem_out):
+        self.running = left
+
+    def drain(self):
+        while self.running:
+            self.tick()
+
+
+def backward_kernel(
+    n_nodes,
+    n_grp,
+    count,
+    mask_ref,
+    targets_ref,
+    stats_ref,
+    hid_h,
+    pre_h,
+    featb_h,
+    board_b_h,
+    neigh_b_h,
+    comb1_b_h,
+    st_h,
+    dnum_h,
+    dz_h,
+    agg_h,
+    gfeat_h,
+    summed_h,
+    small_ref,
+    hid,
+    pre,
+    featb,
+    board_b,
+    neigh_b,
+    comb1_b,
+    spread_t,
+    dnum,
+    dz,
+    agg,
+    picker_t,
+    out_slots,
+    in_slots,
+    chain,
+    tmp,
+    dpre,
+    dh,
+    grad,
+    out,
+    arrive,
+    land,
+    share_l,
+    share_z,
+    share_x,
+    small,
+    load_sem,
+    store_sem,
+    slot_send,
+    slot_recv,
+    up_send,
+    down_send,
+    chain_recv,
+    job_send,
+    job_recv,
+    share_send,
+    share_recv,
+):
     place = Place(n_nodes, n_grp)
-    rows = grad.shape[0] // count
-    loads = []
-    for j in range(count):
-        at = pl.ds(j * rows, rows)
-        load = pltpu.make_async_copy(grad_hbm.at[at], grad.at[at], sem_in.at[j])
-        load.start()
-        loads.append(load)
-    barrier(place, ("c", "x", "y", "z"))
+    z, low = place.at["z"], place.at["l"]
+    layer = place.size["l"]
+    rows, width = hid.shape
+    layer_slots = spread_t.shape[2]
+    cap = layer_slots // layer
+    part = width // CHUNKS
+
+    loads = {}
+    for i, (name, src, dst) in enumerate(
+        (
+            ("dnum", dnum_h, dnum),
+            ("hid", hid_h, hid),
+            ("agg", agg_h, agg),
+            ("dz", dz_h, dz),
+            ("spread_t", st_h, spread_t),
+            ("comb1_b", comb1_b_h, comb1_b),
+            ("pre", pre_h, pre),
+            ("neigh_b", neigh_b_h, neigh_b),
+            ("featb", featb_h, featb),
+            ("board_b", board_b_h, board_b),
+        )
+    ):
+        loads[name] = pltpu.make_async_copy(src, dst, load_sem.at[i])
+        loads[name].start()
+    barrier(place, ("l", "z", "x"))
+    stores = []
+
+    def store(src, dst):
+        copy = pltpu.make_async_copy(src, dst, store_sem.at[len(stores)])
+        copy.start()
+        stores.append(copy)
+
+    mask = mask_ref[...] > 0.5
+
+    def source(which):
+        flip = z // 2
+        inner = z * (1 - 2 * flip) + (LINE - 1) * flip
+        index = ORDER[0][which] * (1 - inner) + ORDER[1][which] * inner
+        return index * (1 - 2 * flip) + (LINE - 1) * flip
+
+    def cols(k):
+        return pl.ds(pl.multiple_of(k * part, part), part)
+
+    def slot_copy(dst, k, far, index, device):
+        at = (dst * CHUNKS + k) * (layer - 1) + far
+        return remote(
+            out_slots.at[dst, k, pl.ds(pl.multiple_of(index * cap, cap), cap)],
+            in_slots.at[dst, k, pl.ds(pl.multiple_of(low * cap, cap), cap)],
+            slot_send.at[at],
+            slot_recv.at[at],
+            device,
+        )
+
+    def back(dst, k):
+        out_slots[dst, k] = jnp.dot(
+            picker_t[dst], dnum[:, cols(k)], preferred_element_type=F32
+        ).astype(BF16)
+        for far, index, device in place.others("l"):
+            slot_copy(dst, k, far, index, device).start()
+        own = pl.ds(pl.multiple_of(low * cap, cap), cap)
+        in_slots[dst, k, own] = out_slots[dst, k, own]
+
+    def child_sums(dst, k):
+        for far, index, device in place.others("l"):
+            slot_copy(dst, k, far, index, device).wait_recv()
+        tmp[...] = jnp.dot(spread_t[dst], in_slots[dst, k], preferred_element_type=F32)
+
+    def up_copy(dst, k):
+        at = dst * CHUNKS + k
+        return remote(
+            chain.at[dst, k],
+            chain.at[dst, k],
+            up_send.at[at],
+            chain_recv.at[at],
+            place.member("z", z + 1),
+        )
+
+    def down_copy(dst, k, last):
+        slot = LINE if last else dst
+        return remote(
+            chain.at[dst, k],
+            chain.at[slot, k],
+            down_send.at[dst * CHUNKS + k],
+            chain_recv.at[slot * CHUNKS + k],
+            place.member("z", z - 1),
+        )
+
+    def arrived(slot, k):
+        remote(
+            chain.at[slot, k],
+            chain.at[slot, k],
+            up_send.at[0],
+            chain_recv.at[slot * CHUNKS + k],
+            place.member("z", lax.rem(z + 1, LINE)),
+        ).wait_recv()
+
+    def hand_on(dst, k):
+        child_sums(dst, k)
+
+        @pl.when(dst > z)
+        def _():
+            @pl.when(z > 0)
+            def _():
+                up_copy(dst, k).wait_recv()
+                chain[dst, k] = (chain[dst, k].astype(F32) + tmp[...]).astype(BF16)
+
+            @pl.when(z == 0)
+            def _():
+                chain[dst, k] = tmp[...].astype(BF16)
+
+            up_copy(dst, k).start()
+
+        @pl.when(dst < z)
+        def _():
+            @pl.when(z < LINE - 1)
+            def _():
+                down_copy(dst, k, False).wait_recv()
+                chain[dst, k] = (chain[dst, k].astype(F32) + tmp[...]).astype(BF16)
+
+            @pl.when(z == LINE - 1)
+            def _():
+                chain[dst, k] = tmp[...].astype(BF16)
+
+            @pl.when(dst == z - 1)
+            def _():
+                down_copy(dst, k, True).start()
+
+            @pl.when(dst < z - 1)
+            def _():
+                down_copy(dst, k, False).start()
+
+    n_rows = grad.shape[0]
+    job_rows = n_rows // count
     per_job = job_sems(n_nodes, n_grp)
+    line = Line()
 
     def job(j):
-        at = pl.ds(j * rows, rows)
-        loads[j].wait()
+        at = pl.ds(j * job_rows, job_rows)
         yield from reduce_job(
             place,
             ("x", "y", "z") if j % 2 == 0 else ("y", "x", "z"),
-            j * rows,
-            rows,
+            j * job_rows,
+            job_rows,
             grad,
             out,
             arrive.at[at],
-            land.at[pl.ds(j * 2 * rows, 2 * rows)],
-            send,
-            recv,
+            land.at[at],
+            job_send,
+            job_recv,
             j * per_job,
         )
-        store = pltpu.make_async_copy(out.at[at], out_hbm.at[at], sem_out.at[j])
-        store.start()
-        stores.append(store)
-
-    stores = []
-    run_jobs([job(j) for j in range(count)], 2)
-    for store in stores:
-        store.wait()
-
-
-def all_reduce(grads, n_nodes, n_grp):
-    rows, width = grads.shape
-    count = max(1, min(8, rows * 2 // (16 * n_nodes * n_grp)))
+        store(out.at[at], summed_h.at[at])
+
+    @pl.loop(0, LINE)
+    def _(src):
+        at = pl.ds(pl.multiple_of(src * layer_slots, layer_slots), layer_slots)
+        ids = lax.broadcasted_iota(jnp.int32, (layer_slots, rows), 1)
+        picker_t[src] = jnp.where(ids == targets_ref[at, :], 1.0, 0.0).astype(BF16)
+
+    loads["dnum"].wait()
+
+    @pl.loop(0, CHUNKS)
+    def _(k):
+        for which in (3, 2):
+            back(source(which), k)
+
+    @pl.loop(0, CHUNKS)
+    def _(k):
+        for which in (1, 0):
+            back(source(which), k)
+
+    loads["spread_t"].wait()
+
+    def chain_pair(k):
+        hand_on(source(3), k)
+        hand_on(source(2), k)
+
+    chain_pair(0)
+    for name in ("hid", "agg", "dz"):
+        loads[name].wait()
+
+    def comb_grad(left, first):
+        @pl.loop(0, CHUNKS)
+        def _(k):
+            grad[pl.ds(first, width), cols(k)] = dot_tn(left[...], dz[:, cols(k)]).astype(BF16)
+
+    comb_grad(hid, 0)
+    comb_grad(agg, width)
+    small[...] = jnp.zeros_like(small)
+    small[1:2, :] = jnp.sum(dz[...].astype(F32), axis=0, keepdims=True)
+    small[2:3, :] = jnp.broadcast_to(stats_ref[0:1, 0:1], (1, width))
+    waiting = [job(j) for j in range(count)]
+    half = count // 2
+
+    def advance():
+        line.tick()
+        if len(waiting) > count - half:
+            line.add(waiting.pop(0))
+
+    advance()
+    chain_pair(1)
+    advance()
+    loads["comb1_b"].wait()
+
+    @pl.loop(0, CHUNKS)
+    def _(k):
+        dh[:, cols(k)] = dot_nt(dz[...], comb1_b[cols(k), :])
+
+    for k in range(2, CHUNKS):
+        chain_pair(k)
+        advance()
+    for k in range(CHUNKS):
+        hand_on(source(1), k)
+        advance()
+    for name in ("pre", "neigh_b", "featb", "board_b"):
+        loads[name].wait()
+
+    def own(k):
+        child_sums(z, k)
+
+        @pl.when(z > 0)
+        def _():
+            arrived(z, k)
+            tmp[...] += chain[z, k].astype(F32)
+
+        @pl.when(z < LINE - 1)
+        def _():
+            arrived(LINE, k)
+            tmp[...] += chain[LINE, k].astype(F32)
+
+        down = (tmp[...] * gelu_slope(pre[:, cols(k)])).astype(BF16)
+        dpre[:, cols(k)] = down
+        small[0:1, cols(k)] = jnp.sum(down.astype(F32), axis=0, keepdims=True)
+        grad[pl.ds(2 * width, width), cols(k)] = dot_tn(hid[...], down).astype(BF16)
+        dh[...] += dot_nt(down, neigh_b[:, cols(k)])
+
+    for k in range(CHUNKS):
+        own(k)
+        advance()
+    while len(waiting) > count - half:
+        advance()
+
+    def tail_job():
+        if waiting:
+            line.add(waiting.pop(0))
+
+    quarter = (count - half) // 2
+    for _ in range(quarter):
+        tail_job()
+    share = Share(place, (share_l, share_z, share_x), share_send, share_recv)
+    share.start(0, small[...])
+    last = dh[...].astype(BF16)
+    dpre[...] = jnp.where(mask, last, jnp.zeros_like(last))
+    pre[...] = last.astype(F32)
+
+    @pl.loop(0, CHUNKS)
+    def _(k):
+        grad[pl.ds(3 * width, width), cols(k)] = dot_tn(featb[...], dpre[:, cols(k)]).astype(BF16)
+
+    line.tick()
+    while waiting:
+        tail_job()
+    share.start(1, share.finish(0))
+
+    @pl.loop(0, CHUNKS)
+    def _(k):
+        pre[:, cols(k)] = jnp.where(
+            mask, dot_nt(dpre[...], board_b[cols(k), :]), pre[:, cols(k)]
+        )
+
+    store(pre, gfeat_h)
+    line.tick()
+    share.start(2, share.finish(1))
+    line.tick()
+    small_ref[...] = share.finish(2)
+    line.drain()
+
+    @pl.loop(0, LINE * CHUNKS)
+    def _(i):
+        dst = i // CHUNKS
+        k = lax.rem(i, CHUNKS)
+
+        @pl.when(dst > z)
+        def _():
+            up_copy(dst, k).wait_send()
+
+        @pl.when(dst < z)
+        def _():
+            down_copy(dst, k, False).wait_send()
+
+        for far, index, device in place.others("l"):
+            slot_copy(dst, k, far, index, device).wait_send()
+
+    for copy in stores:
+        copy.wait()
+
+
+def backward_pass(n_nodes, n_grp, mask, targets, stats, hid, pre, featb, board_b, neigh_b, comb1_b, st, dnum, dz, agg):
+    rows, width = hid.shape
+    layer = n_nodes // LINE
+    layer_slots = st.shape[2]
+    part = width // CHUNKS
+    n_rows = 4 * width
+    count = max(2, min(8, n_rows * 2 // (16 * n_nodes * n_grp)))
+    dma = pltpu.SemaphoreType.DMA
+    big = pl.BlockSpec(memory_space=pl.ANY)
+    vmem = pl.BlockSpec(memory_space=pltpu.VMEM)
     sems = count * job_sems(n_nodes, n_grp)
+    pieces = LINE * CHUNKS
     return pl.pallas_call(
-        functools.partial(reduce_kernel, n_nodes, n_grp, count),
-        out_shape=jax.ShapeDtypeStruct((rows, width), BF16),
-        in_specs=[pl.BlockSpec(memory_space=pl.ANY)],
-        out_specs=pl.BlockSpec(memory_space=pl.ANY),
+        functools.partial(backward_kernel, n_nodes, n_grp, count),
+        out_shape=[
+            jax.ShapeDtypeStruct((rows, width), F32),
+            jax.ShapeDtypeStruct((n_rows, width), BF16),
+            jax.ShapeDtypeStruct((8, width), F32),
+        ],
+        in_specs=[vmem, vmem, vmem] + [big] * 10,
+        out_specs=[big, big, vmem],
         scratch_shapes=[
             pltpu.VMEM((rows, width), BF16),
+            pltpu.VMEM((rows, width), F32),
             pltpu.VMEM((rows, width), BF16),
-            pltpu.VMEM((rows, width // 2), BF16),
-            pltpu.VMEM((2 * rows, width // 2), BF16),
-            pltpu.SemaphoreType.DMA((sems,)),
-            pltpu.SemaphoreType.DMA((sems,)),
-            pltpu.SemaphoreType.DMA((count,)),
-            pltpu.SemaphoreType.DMA((count,)),
+            pltpu.VMEM((width, width), BF16),
+            pltpu.VMEM((width, width), BF16),
+            pltpu.VMEM((width, width), BF16),
+            pltpu.VMEM((LINE, rows, layer_slots), BF16),
+            pltpu.VMEM((rows, width), BF16),
+            pltpu.VMEM((rows, width), BF16),
+            pltpu.VMEM((rows, width), BF16),
+            pltpu.VMEM((LINE, layer_slots, rows), BF16),
+            pltpu.VMEM((LINE, CHUNKS, layer_slots, part), BF16),
+            pltpu.VMEM((LINE, CHUNKS, layer_slots, part), BF16),
+            pltpu.VMEM((LINE + 1, CHUNKS, rows, part), BF16),
+            pltpu.VMEM((rows, part), F32),
+            pltpu.VMEM((rows, width), BF16),
+            pltpu.VMEM((rows, width), F32),
+            pltpu.VMEM((n_rows, width), BF16),
+            pltpu.VMEM((n_rows, width), BF16),
+            pltpu.VMEM((n_rows, width // 2), BF16),
+            pltpu.VMEM((n_rows, width // 2), BF16),
+            pltpu.VMEM((layer, 8, width), F32),
+            pltpu.VMEM((LINE, 8, width), F32),
+            pltpu.VMEM((n_grp, 8, width), F32),
+            pltpu.VMEM((8, width), F32),
+            dma((10,)),
+            dma((count + 1,)),
+            dma((pieces * (layer - 1),)),
+            dma((pieces * (layer - 1),)),
+            dma((pieces,)),
+            dma((pieces,)),
+            dma((pieces + CHUNKS,)),
+            dma((sems,)),
+            dma((sems,)),
+            dma((share_sems(n_nodes, n_grp),)),
+            dma((share_sems(n_nodes, n_grp),)),
         ],
         compiler_params=pltpu.CompilerParams(
-            vmem_limit_bytes=48 * MIB, collective_id=1, has_side_effects=True
+            vmem_limit_bytes=62 * MIB, collective_id=3, has_side_effects=True
         ),
-        name="sum_gradients",
-    )(grads)
+        name="backward_pass",
+    )(mask, targets, stats, hid, pre, featb, board_b, neigh_b, comb1_b, st, dnum, dz, agg)
 
 
 def on_device(
@@ -858,10 +1204,8 @@
     rows, width = feats.shape
     peers = recv_rows.shape[2]
     cap = recv_rows.shape[3]
-    layer = n_nodes // LINE
     slots = peers * cap
     mask = type_mask[0].astype(F32).reshape(rows, 1)
-    board = mask > 0.5
     keys = ((edge_slot[0] * rows + edge_child[0]) * 16 + edge_weight[0]).reshape(1, -1)
     targets = recv_rows[0, 0].reshape(1, slots)
     embed, hidden, pre, featb, pbl, qwl, cwl1, spread_t, dnum, dzb, aggb, stats = forward_pass(
@@ -878,45 +1222,33 @@
         combine_bias.reshape(1, width),
         out_cot[0],
     )
-    board_sq = stats[0, 0]
-    scale = stats[8, 0]
-    joined = jnp.concatenate([hidden, aggb], axis=1)
-    grad_comb = dot_tn(joined, dzb).astype(BF16)
-    grad_cbias = jnp.sum(dzb.astype(F32), axis=0)
-    picker = (targets[0][None, :] == jnp.arange(rows, dtype=jnp.int32)[:, None]).astype(BF16)
-    back_slots = dot_tn(picker, dnum).astype(BF16).reshape(LINE, layer, cap, width)
-    layers = [[i * layer + j for j in range(layer)] for i in range(LINE)]
-    lines = [[i * layer + j for i in range(LINE)] for j in range(layer)]
-    returned = lax.all_to_all(
-        back_slots, "nodes", split_axis=1, concat_axis=1, tiled=True, axis_index_groups=layers
-    ).reshape(LINE, layer * cap, width)
-    partial = jnp.einsum("zcs,zsd->zcd", spread_t, returned, preferred_element_type=F32)
-    dmsg = lax.psum_scatter(
-        partial, "nodes", scatter_dimension=0, axis_index_groups=lines, tiled=False
+    grad_feats, summed, small = backward_pass(
+        n_nodes,
+        n_grp,
+        mask,
+        targets.reshape(slots, 1),
+        stats,
+        hidden,
+        pre,
+        featb,
+        pbl,
+        qwl,
+        cwl1,
+        spread_t,
+        dnum,
+        dzb,
+        aggb,
     )
-    dpre = (dmsg * gelu_slope(pre)).astype(BF16)
-    grad_qbias = jnp.sum(dpre.astype(F32), axis=0)
-    grad_neigh = dot_tn(hidden, dpre).astype(BF16)
-    dhid = (dot_nt(dzb, cwl1) + dot_nt(dpre, qwl)).astype(BF16)
-    dproj = jnp.where(board, dhid, jnp.zeros_like(dhid))
-    grad_board = dot_tn(featb, dproj).astype(BF16)
-    grad_feats = jnp.where(board, dot_nt(dproj, pbl), dhid.astype(F32))
-    small = lax.psum(
-        jnp.concatenate([grad_qbias, grad_cbias, jnp.full((width,), board_sq)]), ("nodes", "grp")
-    )
-    penalty = small[2 * width] * scale
-    summed = all_reduce(
-        jnp.concatenate([grad_comb, grad_neigh, grad_board], axis=0), n_nodes, n_grp
-    )
+    penalty = small[2, 0] * stats[8, 0]
     return (
         embed[None],
         penalty,
         grad_feats[None],
         summed[3 * width :].astype(F32),
         summed[2 * width : 3 * width].astype(F32),
-        small[:width],
+        small[0],
         summed[: 2 * width].astype(F32),
-        small[width : 2 * width],
+        small[1],
     )
 
 

time: 527 us -> 304 us (0.58)
  waiting for transfers between devices: 135 us -> 0 us
  blocking collectives: 92.8 us -> 0 us
  Pallas kernels: 229 us -> 277 us
  matrix products: 24.3 us -> 0 us
  between operations: 16.6 us -> 3.1 us
  other arithmetic: 20.8 us -> 13.8 us
    reduce_scatter x1 -> x0, waiting for transfers between devices: 135 us -> none  [on_device(): lax.psum_scatter(partial, 'nodes', scatter_dimension=0, axis_index_groups...]
    pallas_call x1, Pallas kernels: 85.7 us -> 180 us  [backward_pass(): pl.pallas_call(functools.partial(backward_kernel, n_nodes, n_grp, count),...]
    all_to_all x1 -> x0, blocking collectives: 51.5 us -> none  [on_device(): lax.all_to_all(back_slots, 'nodes', split_axis=1, concat_axis=1, tiled=Tr...]
    pallas_call x1, Pallas kernels: 143 us -> 97.4 us  [forward_pass(): pl.pallas_call(functools.partial(forward_kernel, n_nodes, n_grp), out_sha...]
    psum x1 -> x0, blocking collectives: 41.4 us -> none  [on_device(): lax.psum(jnp.concatenate([grad_qbias, grad_cbias, jnp.full((width,), boar...]
    dot_general x8 -> x0, matrix products: 24.3 us -> none  [the longest x4 12 us: dot_tn(): lax.dot_general(left, right, (((0,), (0,)), ((), ())), preferred_element_...]
  transfers between devices with their start and end apart: 1 -> 0, of which waited for: 1 -> 0; matrix products, arithmetic and copies ran while one was open for 2% -> 0% of each run, Pallas kernels for 0% -> 0%
where the time goes in v3:
time: 304 us
  Pallas kernels  277 us (91%)
  other arithmetic  13.8 us (5%)
  local copies, waits for them, and re-layouts  9.69 us (3%)
  between operations  3.1 us (1%)
    pallas_call x1, Pallas kernels, backward_pass(): pl.pallas_call(functools.partial(backward_kernel, n_nodes, n_grp, count),...  180 us
    pallas_call x1, Pallas kernels, forward_pass(): pl.pallas_call(functools.partial(forward_kernel, n_nodes, n_grp), out_sha...  97.4 us
    convert_element_type x1, other arithmetic, on_device(): summed[2 * width:3 * width].astype(F32)  6.83 us

profile of v3, /device:TPU:0, one launch (start us, length us, event | category | flops | bytes accessed | tf_op | source)
XLA Modules:
  0.0 303.8 jit_solution(14181184370197569488)
XLA Ops:
  0.6 0.7 convert_bitcast_fusion
  1.3 0.9 copy.20.mask_ref
  2.2 1.8 multiply_add_fusion.keys_ref
  4.0 0.0 copy-start.3
  4.0 97.4 %forward_pass.1 = (f32[512,1024]{1,0:T(8,128)}, bf16[512,1024]{1,0:T(8,128)(2,1)}, f32[512,1024]{1,0:T(8,128)}, bf16[512,1024]{1,0:T(8,128)(2,1)}, bf16[1024,102...) custom-call(f32[512,1024]{1,0:T(8,128)} %bitcast.13, ...), custom_call_target="tpu_custom_call" | custom-call | tf_op jit(solution)/shard_map/forward_pass/pallas_call | solution.py:577
  101.4 0.0 copy-done.3
  101.4 1.3 copy.22.targets_ref
  102.8 179.8 %backward_pass.1 = (f32[512,1024]{1,0:T(8,128)}, bf16[4096,1024]{1,0:T(8,128)(2,1)}, f32[8,1024]{1,0:T(8,128)}) custom-call(f32[512,1]{1,0:T(8,128)} %copy.20.mask_ref, s32[2048,1]{1,0:T(8,128)} %copy.22.targets_ref, f32[16,128]{1,0:T(8,128)} %get-tuple-element.24.stats_ref, bf16[512,1024]{1,0:T(8,128)(2,1)} %get-tuple-element.25.hid_h, ...), custom_call_target="tpu_custom_call" | custom-call | tf_op jit(solution)/shard_map/backward_pass/pallas_call | solution.py:1133
  282.6 1.2 slice.21
  283.8 1.2 slice.22
  286.3 0.0 copy-start
  286.3 6.8 %slice_convert_fusion.1 = (f32[1024,1024]{1,0:T(8,128)}, f32[1024,1024]{1,0:T(8,128)}) fusion(bf16[4096,1024]{1,0:T(8,128)(2,1)} %get-tuple-element.37), kind=kLoop, calls=%fused_computation.1 | loop fusion | flops 2097152 | bytes 12582912 | tf_op jit(solution)/shard_map/convert_element_type | solution.py:1248
  293.1 1.4 fusion
  294.6 0.0 copy-done
  294.6 0.0 copy-start.1
  294.6 4.4 %slice_convert_fusion = f32[2048,1024]{1,0:T(8,128)} fusion(bf16[4096,1024]{1,0:T(8,128)(2,1)S(1)} %copy-done), kind=kLoop, calls=%fused_computation | loop fusion | flops 2097152 | bytes 12582912 | tf_op jit(solution)/shard_map/convert_element_type | solution.py:1250
  299.0 0.0 copy-start.2
  299.0 0.0 copy-done.1
  299.0 1.3 copy.25
  300.3 1.0 copy-done.2
  301.3 1.3 copy.26
Async XLA Ops:
  4.0 97.4 %copy-start.3 = (s32[1,1,16,128]{3,2,1,0:T(8,128)S(1)}, s32[1,1,16,128]{3,2,1,0:T(8,128)}, u32[]{:S(2)}) copy-start(s32[1,1,16,128]{3,2,1,0:T(8,128)} %param.17) | copy-start | bytes 24580
  286.3 8.3 %copy-start = (bf16[4096,1024]{1,0:T(8,128)(2,1)S(1)}, bf16[4096,1024]{1,0:T(8,128)(2,1)}, u32[]{:S(2)}) copy-start(bf16[4096,1024]{1,0:T(8,128)(2,1)} %get-tuple-element.37) | copy-start | bytes 25165828
  294.6 4.4 %copy-start.1 = (f32[512,1024]{1,0:T(8,128)S(1)}, f32[512,1024]{1,0:T(8,128)}, u32[]{:S(2)}) copy-start(f32[512,1024]{1,0:T(8,128)} %get-tuple-element.23) | copy-start | bytes 6291460
  299.0 2.3 copy-start.2
